TPU v7x, 32 devices: a whole 2x2x4 slice. The times are simulated.
32 devices in a mesh: dp: 8 (over z, x), ctx: 4 (over y, core).
Axes of the slice: x: 2, y: 2, z: 4, core: 2. Of those that a mesh axis runs over, the one named last changes fastest.
Arguments:
- prompt_q: bfloat16 [8, 512, 4096], P('dp', 'ctx'), may hold values from -260 to 260
- prompt_k: bfloat16 [8, 512, 512], P('dp', 'ctx'), may hold values from -8 to 8
- prompt_v: bfloat16 [8, 512, 512], P('dp', 'ctx'), may hold values from -12 to 12
- prompt_len: int32 [8], P('dp'), may hold values from 256 to 512
- resp_q: bfloat16 [8, 128, 4096], P('dp', 'ctx'), may hold values from -260 to 260
- resp_k: bfloat16 [8, 128, 512], P('dp', 'ctx'), may hold values from -6 to 6
- resp_v: bfloat16 [8, 128, 512], P('dp', 'ctx'), may hold values from -12 to 12
- resp_len: int32 [8, 8], P('dp', 'ctx'), may hold values from 1 to 16
- resp_resid: bfloat16 [8, 128, 4096], P('dp', 'ctx'), may hold values from -4 to 4
- norm_gain: float32 [4096], replicated, may hold values from 0.5 to 1.5
- gate_weight: bfloat16 [4096, 14336], P('dp', 'ctx'), may hold values from -0.09375 to 0.09375
- up_weight: bfloat16 [4096, 14336], P('dp', 'ctx'), may hold values from -0.09375 to 0.09375
Outputs:
- prompt_attn: bfloat16 [8, 512, 4096], P('dp', 'ctx')
- resp_hidden: bfloat16 [8, 128, 14336], P('dp', None, 'ctx')
All inputs are finite; a program needn't handle non-finite values.
Results may differ from a plain program's by a relative error of at most 0.012.
Values may be sent and summed in bfloat16 or wider, within the bound.
A program may use at most 128 MiB of HBM per device.

v0:
```python
import jax
import jax.numpy as jnp
from jax import lax
from jax.sharding import PartitionSpec as P

QUERY_HEADS = 32
KEY_VALUE_HEADS = 4
HEAD_SIZE = 128
RLEN = 16


def to_heads(token_rows):
    group_count = token_rows.shape[0]
    return (
        token_rows.reshape(group_count, KEY_VALUE_HEADS, QUERY_HEADS // KEY_VALUE_HEADS, HEAD_SIZE)
        .transpose(1, 2, 0, 3)
        .reshape(KEY_VALUE_HEADS, QUERY_HEADS // KEY_VALUE_HEADS * group_count, HEAD_SIZE)
    )


def from_heads(head_rows, group_count):
    return (
        head_rows.reshape(KEY_VALUE_HEADS, QUERY_HEADS // KEY_VALUE_HEADS, group_count, HEAD_SIZE)
        .transpose(2, 0, 1, 3)
        .reshape(group_count, QUERY_HEADS * HEAD_SIZE)
    )


def fresh_state(group_count):
    token_rows = QUERY_HEADS // KEY_VALUE_HEADS * group_count
    return (
        jnp.full((KEY_VALUE_HEADS, token_rows), -1e30, jnp.float32),
        jnp.zeros((KEY_VALUE_HEADS, token_rows), jnp.float32),
        jnp.zeros((KEY_VALUE_HEADS, token_rows, HEAD_SIZE), jnp.float32),
    )


def absorb(state, queries, key_rows, value_rows, start, visible_mask_builder):
    length = key_rows.shape[0]
    attention_block = length
    while attention_block > 512 and attention_block % 2 == 0:
        attention_block = attention_block // 2

    def one_block(index, carry):
        top, total, mixed = carry
        offset = index * attention_block
        key_matrix = (
            lax.dynamic_slice_in_dim(key_rows, offset, attention_block, 0)
            .reshape(attention_block, KEY_VALUE_HEADS, HEAD_SIZE)
            .transpose(1, 0, 2)
        )
        values = (
            lax.dynamic_slice_in_dim(value_rows, offset, attention_block, 0)
            .reshape(attention_block, KEY_VALUE_HEADS, HEAD_SIZE)
            .transpose(1, 0, 2)
        )
        key_position = start + offset + jnp.arange(attention_block, dtype=jnp.int32)
        grouped_heads = jnp.tile(
            visible_mask_builder(key_position), (QUERY_HEADS // KEY_VALUE_HEADS, 1)
        )[None]
        scores = jnp.einsum(
            "kqd,ktd->kqt", queries, key_matrix, preferred_element_type=jnp.float32
        ) * HEAD_SIZE ** (-0.5)
        scores = jnp.where(grouped_heads, scores, -1e30)
        newtop = jnp.maximum(top, jnp.max(scores, axis=-1))
        weights = jnp.where(grouped_heads, jnp.exp(scores - newtop[..., None]), 0.0)
        factor = jnp.exp(top - newtop)
        total = total * factor + jnp.sum(weights, axis=-1)
        mixed = mixed * factor[..., None] + jnp.einsum(
            "kqt,ktd->kqd", weights.astype(jnp.bfloat16), values, preferred_element_type=jnp.float32
        )
        return (newtop, total, mixed)

    return lax.fori_loop(0, length // attention_block, one_block, state)


def finish(state, group_count):
    top, total, mixed = state
    return from_heads(mixed / total[..., None], group_count).astype(jnp.bfloat16)


def local(
    prompt_q,
    prompt_k,
    prompt_v,
    prompt_len,
    resp_q,
    resp_k,
    resp_v,
    resp_len,
    resp_resid,
    norm_gain,
    gate_weight,
    up_weight,
):
    whole_gate, whole_up = (
        lax.all_gather(gate_weight, "dp", axis=0, tiled=True),
        lax.all_gather(up_weight, "dp", axis=0, tiled=True),
    )
    ptok = prompt_q.shape[1]
    rtok = resp_q.shape[1]
    here = lax.axis_index("ctx")
    limit = prompt_len[0]
    lens = resp_len[0]
    qpos = here * ptok + jnp.arange(ptok, dtype=jnp.int32)
    prompt_heads = to_heads(prompt_q[0])
    resp_heads = to_heads(resp_q[0])

    def prompt_visible(key_position):
        return (key_position[None, :] <= qpos[:, None]) & (key_position[None, :] < limit)

    def resp_prompt_visible(key_position):
        return jnp.broadcast_to((key_position < limit)[None, :], (rtok, key_position.shape[0]))

    token_rows = jnp.arange(rtok, dtype=jnp.int32)
    slot_r = token_rows // RLEN
    place_r = token_rows % RLEN

    def own_visible(key_position):
        slot_t = key_position // RLEN
        place_t = key_position % RLEN
        bound_t = jnp.where(slot_t == 0, lens[0], lens[1])
        return (
            (slot_r[:, None] == slot_t[None, :])
            & (place_t[None, :] <= place_r[:, None])
            & (place_t[None, :] < bound_t[None, :])
        )

    resp_state = absorb(fresh_state(rtok), resp_heads, resp_k[0], resp_v[0], 0, own_visible)
    pieces = (
        lax.all_gather(prompt_k[0], "ctx", axis=0, tiled=True),
        lax.all_gather(prompt_v[0], "ctx", axis=0, tiled=True),
    )
    prompt_state = absorb(
        fresh_state(ptok), prompt_heads, pieces[0], pieces[1], jnp.int32(0), prompt_visible
    )
    pieces = (
        lax.all_gather(prompt_k[0], "ctx", axis=0, tiled=True),
        lax.all_gather(prompt_v[0], "ctx", axis=0, tiled=True),
    )
    resp_state = absorb(
        resp_state, resp_heads, pieces[0], pieces[1], jnp.int32(0), resp_prompt_visible
    )
    prompt_out = finish(prompt_state, ptok)
    resp_attn = finish(resp_state, rtok)
    stream = resp_resid[0].astype(jnp.float32) + resp_attn.astype(jnp.float32)
    scale = lax.rsqrt(jnp.mean(stream * stream, axis=-1, keepdims=True) + 1e-05)
    normed = (stream * scale * norm_gain).astype(jnp.bfloat16)
    grouped_rows = lax.all_gather(normed, "ctx", axis=0, tiled=True)
    gate = jnp.dot(grouped_rows, whole_gate, preferred_element_type=jnp.float32)
    up = jnp.dot(grouped_rows, whole_up, preferred_element_type=jnp.float32)
    hidden = (jax.nn.silu(gate) * up).astype(jnp.bfloat16)
    return (prompt_out[None], hidden[None])


def solution(mesh):
    return jax.shard_map(
        local,
        mesh=mesh,
        in_specs=(
            P("dp", "ctx", None),
            P("dp", "ctx", None),
            P("dp", "ctx", None),
            P("dp"),
            P("dp", "ctx", None),
            P("dp", "ctx", None),
            P("dp", "ctx", None),
            P("dp", "ctx"),
            P("dp", "ctx", None),
            P(),
            P("dp", "ctx"),
            P("dp", "ctx"),
        ),
        out_specs=(P("dp", "ctx", None), P("dp", None, "ctx")),
        check_vma=False,
    )
```

profile of v0, /device:TPU:0, one launch (start us, length us, event | category | flops | bytes accessed | tf_op | source)
XLA Modules:
  0.0 1195.2 jit_solution(10676516993271004699)
XLA Ops:
  7.2 0.0 copy-start.4
  7.2 0.0 all-gather.6.cloned.1.call-start
  7.2 1.3 fusion.49
  8.6 1.3 fusion.39
  9.9 0.1 and_and_fusion
  10.0 0.1 tile.41
  10.1 1.0 copy.35
  11.1 0.1 copy.28
  11.2 0.8 reshape.292
  12.6 1.0 copy.22
  13.7 8.6 all-gather
  22.3 0.3 copy.23
  22.6 0.0 copy-done.4
  22.6 0.1 copy.24
  22.8 7.3 all-gather.1
  30.1 0.3 copy.25
  30.3 0.2 fusion.50
  30.6 0.5 fusion.8
  31.2 0.6 fusion.11
  31.8 0.5 fusion.14
  32.3 0.0 copy-start.2
  32.3 0.7 fusion.15
  33.0 0.0 copy-start.5
  33.1 0.3 copy.31
  33.4 0.0 copy-done.2
  33.4 0.4 multiply_reduce_fusion
  33.8 1.0 multiply_convert_fusion
  34.9 0.0 all-gather.6.cloned.1.call-update
  34.9 0.0 all-gather.8.cloned.1.call-start
  34.9 0.7 all-gather.8.cloned.1.call-update
  35.6 0.0 copy-start.1
  35.6 0.2 all-gather.10.cloned.1.call-start
  35.9 0.5 all-gather.10.cloned.1.call-update
  36.4 0.1 fusion.28
  36.5 0.2 tile.38
  36.8 0.3 copy.53
  37.1 0.2 copy.34
  37.3 0.4 copy.21
  37.7 1.6 fusion
  39.4 2.1 fusion.1
  41.5 4.1 divide_convert_fusion
  45.6 0.7 copy.27
  46.3 1.3 convert_element_type.65
  47.6 5.1 all-gather.6.cloned.1.call-done
  52.7 560.6 %all-gather.8.cloned.1.call-done = bf16[4096,3584]{1,0:T(8,128)(2,1)} async-done(((bf16[512,3584]{1,0:T(8,128)(2,1)}), bf16[4096,3584]{1,0:T(8,128)(2,1)}) %all-gather.8.cloned.1.call-update) | async-done | bytes 29360144 | tf_op jit(solution)/shard_map/all_gather | solution.py:97
  613.3 12.4 %fusion.51 = f32[128,3584]{1,0:T(8,128)S(1)} fusion(bf16[128,4096]{1,0:T(8,128)(2,1)} %all-gather.6.cloned.1.call-done, bf16[4096,3584]{1,0:T(8,128)(2,1)} %all-gather.8.cloned.1.call-done), kind=kOutput, calls=%fused_computation.78 | convolution fusion | flops 3758096384 | bytes 32243712 | tf_op jit(solution)/shard_map/dot_general | solution.py:150
  625.7 548.2 %all-gather.10.cloned.1.call-done = bf16[4096,3584]{1,0:T(8,128)(2,1)} async-done(((bf16[512,3584]{1,0:T(8,128)(2,1)}), bf16[4096,3584]{1,0:T(8,128)(2,1)}) %all-gather.10.cloned.1.call-update) | async-done | bytes 29360144 | tf_op jit(solution)/shard_map/all_gather | solution.py:98
  1173.9 14.7 %fusion.4 = bf16[1,128,3584]{2,1,0:T(8,128)(2,1)} fusion(bf16[128,4096]{1,0:T(8,128)(2,1)S(1)} %copy-done, bf16[4096,3584]{1,0:T(8,128)(2,1)} %all-gather.10.cloned.1.call-done, f32[128,3584]{1,0:T(8,128)S(1)} %fusion.51), kind=kOutput, calls=%fused_computation.7 | convolution fusion | flops 3760848896 | bytes 33161216 | tf_op jit(solution)/shard_map/dot_general | solution.py:151
  (18 shorter events, 0.2 us)
Async XLA Ops:
  7.2 15.4 %copy-start.4 = (bf16[1,32,512]{2,1,0:T(8,128)(2,1)S(1)}, bf16[1,32,512]{2,1,0:T(8,128)(2,1)}, u32[]{:S(2)}) copy-start(bf16[1,32,512]{2,1,0:T(8,128)(2,1)} %param.18) | copy-start | bytes 98308
  7.2 15.5 %copy-start.3 = (bf16[1,128,512]{2,1,0:T(8,128)(2,1)S(1)}, bf16[1,128,512]{2,1,0:T(8,128)(2,1)}, u32[]{:S(2)}) copy-start(bf16[1,128,512]{2,1,0:T(8,128)(2,1)} %param.14) | copy-start | bytes 393220
  7.2 45.5 %all-gather.6.cloned.1.call-start = ((), (), s32[]{:S(2)}) async-start(), calls=%async_computation | async-start | bytes 1310720 | tf_op jit(solution)/shard_map/all_gather | solution.py:149
  32.3 1.1 copy-start.2
  33.0 0.8 copy-start.5
  34.9 578.4 %all-gather.8.cloned.1.call-start = ((), (), s32[]{:S(2)}) async-start(), calls=%async_computation.1 | async-start | bytes 33030144 | tf_op jit(solution)/shard_map/all_gather | solution.py:97
  35.6 1.4 copy-start.1
  35.6 1138.3 %all-gather.10.cloned.1.call-start = ((), (), s32[]{:S(2)}) async-start(), calls=%async_computation.2 | async-start | bytes 33030144 | tf_op jit(solution)/shard_map/all_gather | solution.py:98
  52.7 1121.3 %copy-start = (bf16[128,4096]{1,0:T(8,128)(2,1)S(1)}, bf16[128,4096]{1,0:T(8,128)(2,1)}, u32[]{:S(2)}) copy-start(bf16[128,4096]{1,0:T(8,128)(2,1)} %all-gather.6.cloned.1.call-done) | copy-start | bytes 3145732
Sparse Core Ops, SparseCore 0:
  35.0 17.6 all-gather.5
  54.2 559.0 all-gather.7
  614.8 559.0 all-gather.9
where the time goes:
time: 1200 us
  waiting for transfers between devices  1120 us (93%)
  matrix products  34.8 us (3%)
  blocking collectives  16 us (1%)
  between operations  14.7 us (1%)
    all_gather x1, waiting for transfers between devices, local(): lax.all_gather(gate_weight, 'dp', axis=0, tiled=True)  561 us
    all_gather x1, waiting for transfers between devices, local(): lax.all_gather(up_weight, 'dp', axis=0, tiled=True)  548 us
  transfers between devices with their start and end apart: 3, of which 3 were waited for; matrix products, arithmetic and copies ran while one was open for 2% of the time, Pallas kernels for 0%

commit v1 on v0

--- a/solution.py
+++ b/solution.py
@@ -93,10 +93,22 @@
     gate_weight,
     up_weight,
 ):
-    whole_gate, whole_up = (
-        lax.all_gather(gate_weight, "dp", axis=0, tiled=True),
-        lax.all_gather(up_weight, "dp", axis=0, tiled=True),
-    )
+    dp = lax.axis_size("dp")
+    inner = 2 if dp % 2 == 0 else 1
+    outer = dp // inner
+    dp_here = lax.axis_index("dp")
+    z, x = dp_here // inner, dp_here % inner
+    depth, width = gate_weight.shape
+    parts = 4 if width % 4 == 0 else 1
+    part = width // parts
+    pair = [(i, i // inner * inner + (i + 1) % inner) for i in range(dp)]
+    mine = [
+        jnp.concatenate(
+            [gate_weight[:, i * part : (i + 1) * part], up_weight[:, i * part : (i + 1) * part]], 1
+        )
+        for i in range(parts)
+    ]
+    others = [lax.ppermute(block, "dp", pair) for block in mine] if inner > 1 else None
     ptok = prompt_q.shape[1]
     rtok = resp_q.shape[1]
     here = lax.axis_index("ctx")
@@ -134,10 +146,6 @@
     prompt_state = absorb(
         fresh_state(ptok), prompt_heads, pieces[0], pieces[1], jnp.int32(0), prompt_visible
     )
-    pieces = (
-        lax.all_gather(prompt_k[0], "ctx", axis=0, tiled=True),
-        lax.all_gather(prompt_v[0], "ctx", axis=0, tiled=True),
-    )
     resp_state = absorb(
         resp_state, resp_heads, pieces[0], pieces[1], jnp.int32(0), resp_prompt_visible
     )
@@ -147,9 +155,41 @@
     scale = lax.rsqrt(jnp.mean(stream * stream, axis=-1, keepdims=True) + 1e-05)
     normed = (stream * scale * norm_gain).astype(jnp.bfloat16)
     grouped_rows = lax.all_gather(normed, "ctx", axis=0, tiled=True)
-    gate = jnp.dot(grouped_rows, whole_gate, preferred_element_type=jnp.float32)
-    up = jnp.dot(grouped_rows, whole_up, preferred_element_type=jnp.float32)
-    hidden = (jax.nn.silu(gate) * up).astype(jnp.bfloat16)
+    rows = grouped_rows.shape[0]
+    columns = jnp.moveaxis(grouped_rows.reshape(rows, outer, inner * depth), 1, 0)
+    groups = [[i * inner + j for i in range(outer)] for j in range(inner)]
+    if outer > 1:
+        columns = lax.all_to_all(columns, "dp", 0, 0, axis_index_groups=groups, tiled=True)
+    columns = columns.reshape(outer * rows, inner, depth)
+    own_columns = lax.dynamic_index_in_dim(columns, x, 1, keepdims=False)
+    other_columns = lax.dynamic_index_in_dim(columns, (x + 1) % inner, 1, keepdims=False)
+    hidden_parts = []
+    for i in range(parts):
+        partial = jnp.dot(own_columns, mine[i], preferred_element_type=jnp.float32)
+        if inner > 1:
+            partial = partial + jnp.dot(
+                other_columns, others[i], preferred_element_type=jnp.float32
+            )
+        partial = partial.reshape(outer, rows, 2 * part)
+        result = lax.dynamic_index_in_dim(partial, z, 0, keepdims=False)
+        for way in (1, -1):
+            arrived = jnp.zeros((rows, 2 * part), jnp.float32)
+            for step in range(outer - 1):
+                target = jnp.clip(z + way * (outer - 1 - step), 0, outer - 1)
+                term = lax.dynamic_index_in_dim(partial, target, 0, keepdims=False)
+                perm = []
+                for source in range(outer):
+                    rank = source if way == 1 else outer - 1 - source
+                    if rank <= step:
+                        perm += [
+                            (source * inner + j, (source + way) * inner + j) for j in range(inner)
+                        ]
+                sent = (term + arrived).astype(jnp.bfloat16)
+                arrived = lax.ppermute(sent, "dp", perm).astype(jnp.float32)
+            result = result + arrived
+        gate, up = result[:, :part], result[:, part:]
+        hidden_parts.append((jax.nn.silu(gate) * up).astype(jnp.bfloat16))
+    hidden = jnp.concatenate(hidden_parts, 1)
     return (prompt_out[None], hidden[None])
 
 

time: 1200 us -> 339 us (0.28)
  waiting for transfers between devices: 1120 us -> 167 us
  starting transfers between devices: 0.3 us -> 70.2 us
  local copies, waits for them, and re-layouts: 8.46 us -> 24.6 us
    all_gather x2 -> x0, waiting for transfers between devices: 1110 us -> none  [the longest x1 561 us: local(): lax.all_gather(gate_weight, 'dp', axis=0, tiled=True)]
    ppermute x0 -> x28, waiting for transfers between devices: none -> 156 us  [the longest x4 88.2 us: local(): lax.ppermute(block, 'dp', pair)]
    ppermute x0 -> x28, starting transfers between devices: none -> 65.3 us  [the longest x24 61.1 us: local(): arrived = lax.ppermute(sent, 'dp', perm).astype(jnp.float32)]
    dot_general x2 -> x8, matrix products: 27.1 us -> 15.2 us  [the longest x4 10.7 us: local(): jnp.dot(other_columns, others[i], preferred_element_type=jnp.float32)]
  transfers between devices with their start and end apart: 3 -> 30, of which waited for: 3 -> 14; matrix products, arithmetic and copies ran while one was open for 2% -> 16% of each run, Pallas kernels for 0% -> 0%
where the time goes in v1:
time: 339 us; the launch traced here: 338 us
  waiting for transfers between devices  167 us (49%)
  starting transfers between devices  70.2 us (21%)
  matrix products  26.8 us (8%)
  local copies, waits for them, and re-layouts  24.6 us (7%)
  other arithmetic  17.6 us (5%)
  blocking collectives  16 us (5%)
  between operations  15.6 us (5%)
    ppermute x4, waiting for transfers between devices, local(): lax.ppermute(block, 'dp', pair)  88.2 us
    ppermute x24, waiting for transfers between devices, local(): arrived = lax.ppermute(sent, 'dp', perm).astype(jnp.float32)  67.5 us
    ppermute x24, starting transfers between devices, local(): arrived = lax.ppermute(sent, 'dp', perm).astype(jnp.float32)  61.1 us
    all_to_all x1, waiting for transfers between devices, local(): lax.all_to_all(columns, 'dp', 0, 0, axis_index_groups=groups, tiled=True)  11.7 us
    dot_general x4, matrix products, local(): jnp.dot(other_columns, others[i], preferred_element_type=jnp.float32)  10.7 us
    all_gather x1, blocking collectives, local(): lax.all_gather(prompt_k[0], 'ctx', axis=0, tiled=True)  8.65 us
    all_gather x1, blocking collectives, local(): lax.all_gather(prompt_v[0], 'ctx', axis=0, tiled=True)  7.31 us
  transfers between devices with their start and end apart: 30, of which 14 were waited for; matrix products, arithmetic and copies ran while one was open for 16% of the time, Pallas kernels for 0%

profile of v1, /device:TPU:0, one launch (start us, length us, event | category | flops | bytes accessed | tf_op | source)
XLA Modules:
  0.0 338.2 jit_solution(1014979487179150268)
XLA Ops:
  13.6 8.6 %all-gather = bf16[1,512,512]{1,2,0:T(8,128)(2,1)S(1)} all-gather(bf16[1,128,512]{1,2,0:T(8,128)(2,1)S(1)} %copy.22), channel_id=2, replica_groups=mesh['dp'=8,'ctx'=4] {'ctx'}, dimensions={1}, use_global_device_ids=true | all-gather | bytes 655360 | tf_op jit(solution)/shard_map/all_gather | solution.py:143
  24.4 7.3 %all-gather.1 = bf16[1,512,512]{1,2,0:T(8,128)(2,1)S(1)} all-gather(bf16[1,128,512]{1,2,0:T(8,128)(2,1)S(1)} %copy.24), channel_id=3, replica_groups=mesh['dp'=8,'ctx'=4] {'ctx'}, dimensions={1}, use_global_device_ids=true | all-gather | bytes 655360 | tf_op jit(solution)/shard_map/all_gather | solution.py:144
  36.5 3.9 %fusion.91 = (bf16[512,896]{1,0:T(8,128)(2,1)S(1)}, bf16[512,896]{1,0:T(8,128)(2,1)S(1)}, bf16[512,896]{1,0:T(8,128)(2,1)S(1)}, bf16[512,896]{1,0:T(8,128)(2,1)S...) fusion(bf16[512,3584]{1,0:T(8,128)(2,1)} %param.22, ...), kind=kLoop, calls=%fused_computation.161 | loop fusion | bytes 14680064 | tf_op jit(solution)/shard_map/slice | solution.py:107
  40.5 1.5 pad_maximum_fusion
  42.0 1.5 collective-permute-start
  43.5 1.4 pad_maximum_fusion.1
  45.6 1.4 pad_maximum_fusion.2
  47.0 1.4 collective-permute-start.14
  48.4 1.4 pad_maximum_fusion.3
  51.1 1.5 copy.38
  52.9 4.9 %fusion = (f32[4,1024]{1,0:T(4,128)S(1)}, f32[4,1024,512]{1,2,0:T(8,128)}) fusion(pred[1024,512]{0,1:T(8,128)(4,1)S(1)} %bitcast.225, bf16[4,1024,128]{2,1,0:T(8,128)(2,1)S(1)} %bitcast.230, bf16[512,4,128]{2,0,1:T(8,128)(2,1)S(1)} %copy.23), kind=kOutput, calls=%fused_computation.2 | convolution fusion | flops 543158272 | bytes 10502144 | tf_op jit(solution)/shard_map/while/body/eval_jaxpr/kqd,ktd->kqt/dot_general | solution.py:61
  57.9 2.4 copy.59
  60.2 4.9 %all-to-all-start = ((bf16[4,128,1024]{2,1,0:T(8,128)(2,1)}), bf16[4,128,1024]{2,1,0:T(8,128)(2,1)}, u32[]{:S(2)}, u32[]{:S(2)}) async-start(bf16[4,128,1024]{2,1,0:T(8,128)(2,1)} %bitcast.231), calls=%async_computation | async-start | bytes 2097152 | tf_op jit(solution)/shard_map/all_to_all | solution.py:162
  65.1 4.7 %fusion.1 = f32[4,1024]{1,0:T(4,128)S(1)} fusion(f32[4,1024,512]{1,2,0:T(8,128)} %get-tuple-element.128, f32[4,1024]{1,0:T(4,128)S(1)} %broadcast_maximum_fusion, pred[1024,512]{0,1:T(8,128)(4,1)S(1)} %bitcast.226), kind=kLoop, calls=%fused_computation.3 | loop fusion | flops 10481664 | bytes 8945664 | tf_op jit(solution)/shard_map/while/body/eval_jaxpr/reduce_sum | solution.py:68
  70.9 4.8 %divide_convert_fusion = bf16[4,1024,128]{2,1,0:T(8,128)(2,1)} fusion(f32[4,1024,512]{1,2,0:T(8,128)S(1)} %copy-done, f32[4,1024]{1,0:T(4,128)S(1)} %broadcast_maximum_fusion, pred[1024,512]{0,1:T(8,128)(4,1)S(1)} %bitcast.227, f32[4,1024]{1,0:T(4,128)S(1)} %get-tuple-element.121, f32[4,1024]{1,0:T(4,128)S(1)} %get-tuple-element.120, ...), kind=kOutput, calls=%fused_computation.13 | convolution fusion | flops 548929536 | bytes 10534912 | tf_op jit(solution)/shard_map/while/body/eval_jaxpr/kqt,ktd->kqd/dot_general | solution.py:69
  75.7 1.9 copy.27
  78.9 11.7 %all-to-all-done = bf16[4,128,1024]{2,1,0:T(8,128)(2,1)} async-done(((bf16[4,128,1024]{2,1,0:T(8,128)(2,1)}), bf16[4,128,1024]{2,1,0:T(8,128)(2,1)}, u32[]{:S(2)}, u32[]{:S(2)}) %all-to-all-start) | async-done | bytes 1048608 | tf_op jit(solution)/shard_map/all_to_all | solution.py:162
  90.6 1.8 reshape.321
  92.5 2.2 constant_dynamic-slice_fusion
  96.1 2.8 convolution_add_fusion.3
  99.0 1.3 collective-permute-start.1
  102.2 22.3 %collective-permute-done.7 = bf16[512,1792]{1,0:T(8,128)(2,1)} collective-permute-done((bf16[512,1792]{1,0:T(8,128)(2,1)}, bf16[512,1792]{1,0:T(8,128)(2,1)}, u32[]{:S(2)}, u32[]{:S(2)}) %collective-permute-start.7) | collective-permute-done | bytes 1835040 | tf_op jit(solution)/shard_map/ppermute | solution.py:111
  124.5 2.6 convolution_add_fusion.2
  127.2 3.5 %collective-permute-start.8 = (bf16[128,1792]{1,0:T(8,128)(2,1)S(1)}, bf16[128,1792]{1,0:T(8,128)(2,1)S(1)}, u32[]{:S(2)}, u32[]{:S(2)}) collective-permute-start(bf16[128,1792]{1,0:T(8,128)(2,1)S(1)} %get-tuple-element.90), channel_id=1, source_target_pairs={{0,8},{4,12},{1,9},{5,13},{2,10},{6,14},{3,11},{7,15}} | collective-permute-start | bytes 1376264 | tf_op jit(solution)/shard_map/ppermute | solution.py:188
  131.9 31.9 %collective-permute-done.14 = bf16[512,1792]{1,0:T(8,128)(2,1)} collective-permute-done((bf16[512,1792]{1,0:T(8,128)(2,1)}, bf16[512,1792]{1,0:T(8,128)(2,1)}, u32[]{:S(2)}, u32[]{:S(2)}) %collective-permute-start.14) | collective-permute-done | bytes 1835040 | tf_op jit(solution)/shard_map/ppermute | solution.py:111
  164.7 2.6 convolution_add_fusion.1
  168.6 34.0 %collective-permute-done.21 = bf16[512,1792]{1,0:T(8,128)(2,1)} collective-permute-done((bf16[512,1792]{1,0:T(8,128)(2,1)}, bf16[512,1792]{1,0:T(8,128)(2,1)}, u32[]{:S(2)}, u32[]{:S(2)}) %collective-permute-start.21) | collective-permute-done | bytes 1835040 | tf_op jit(solution)/shard_map/ppermute | solution.py:111
  202.6 3.5 %collective-permute-start.15 = (bf16[128,1792]{1,0:T(8,128)(2,1)S(1)}, bf16[128,1792]{1,0:T(8,128)(2,1)S(1)}, u32[]{:S(2)}, u32[]{:S(2)}) collective-permute-start(bf16[128,1792]{1,0:T(8,128)(2,1)S(1)} %get-tuple-element.103), channel_id=1, source_target_pairs={{0,8},{4,12},{1,9},{5,13},{2,10},{6,14},{3,11},{7,15}} | collective-permute-start | bytes 1376264 | tf_op jit(solution)/shard_map/ppermute | solution.py:188
  206.1 2.6 convolution_add_fusion
  209.7 1.3 collective-permute-start.22
  211.1 5.9 %collective-permute-done.15 = bf16[128,1792]{1,0:T(8,128)(2,1)S(1)} collective-permute-done((bf16[128,1792]{1,0:T(8,128)(2,1)S(1)}, bf16[128,1792]{1,0:T(8,128)(2,1)S(1)}, u32[]{:S(2)}, u32[]{:S(2)}) %collective-permute-start.15) | collective-permute-done | bytes 458784 | tf_op jit(solution)/shard_map/ppermute | solution.py:188
  217.8 7.6 %collective-permute-done.22 = bf16[128,1792]{1,0:T(8,128)(2,1)S(1)} collective-permute-done((bf16[128,1792]{1,0:T(8,128)(2,1)S(1)}, bf16[128,1792]{1,0:T(8,128)(2,1)S(1)}, u32[]{:S(2)}, u32[]{:S(2)}) %collective-permute-start.22) | collective-permute-done | bytes 458784 | tf_op jit(solution)/shard_map/ppermute | solution.py:188
  225.4 4.4 %collective-permute-start.2 = (bf16[128,1792]{1,0:T(8,128)(2,1)S(1)}, bf16[128,1792]{1,0:T(8,128)(2,1)S(1)}, u32[]{:S(2)}, u32[]{:S(2)}) collective-permute-start(bf16[128,1792]{1,0:T(8,128)(2,1)S(1)} %fusion.37), channel_id=1, source_target_pairs={{0,8},{4,12},{8,16},{12,20},{1,9},{5,13},{9,17},{13,21},{2,10},{6,... | collective-permute-start | bytes 1376264 | tf_op jit(solution)/shard_map/ppermute | solution.py:188
  229.9 1.9 collective-permute-start.9
  231.8 8.9 %collective-permute-done.2 = bf16[128,1792]{1,0:T(8,128)(2,1)S(1)} collective-permute-done((bf16[128,1792]{1,0:T(8,128)(2,1)S(1)}, bf16[128,1792]{1,0:T(8,128)(2,1)S(1)}, u32[]{:S(2)}, u32[]{:S(2)}) %collective-permute-start.2) | collective-permute-done | bytes 458784 | tf_op jit(solution)/shard_map/ppermute | solution.py:188
  240.7 4.4 %collective-permute-start.16 = (bf16[128,1792]{1,0:T(8,128)(2,1)S(1)}, bf16[128,1792]{1,0:T(8,128)(2,1)S(1)}, u32[]{:S(2)}, u32[]{:S(2)}) collective-permute-start(bf16[128,1792]{1,0:T(8,128)(2,1)S(1)} %fusion.27), channel_id=1, source_target_pairs={{0,8},{4,12},{8,16},{12,20},{1,9},{5,13},{9,17},{13,21},{2,10},{6,... | collective-permute-start | bytes 1376264 | tf_op jit(solution)/shard_map/ppermute | solution.py:188
  245.3 1.9 collective-permute-start.23
  247.3 3.3 collective-permute-done.9
  251.4 5.0 %collective-permute-start.3 = (bf16[128,1792]{1,0:T(8,128)(2,1)S(1)}, bf16[128,1792]{1,0:T(8,128)(2,1)S(1)}, u32[]{:S(2)}, u32[]{:S(2)}) collective-permute-start(bf16[128,1792]{1,0:T(8,128)(2,1)S(1)} %get-tuple-element.66), channel_id=1, source_target_pairs={{0,8},{4,12},{8,16},{12,20},{16,24},{20,28},{1,9},{5,13},{9,17},{1... | collective-permute-start | bytes 1376264 | tf_op jit(solution)/shard_map/ppermute | solution.py:188
  256.4 3.9 %collective-permute-done.16 = bf16[128,1792]{1,0:T(8,128)(2,1)S(1)} collective-permute-done((bf16[128,1792]{1,0:T(8,128)(2,1)S(1)}, bf16[128,1792]{1,0:T(8,128)(2,1)S(1)}, u32[]{:S(2)}, u32[]{:S(2)}) %collective-permute-start.16) | collective-permute-done | bytes 458784 | tf_op jit(solution)/shard_map/ppermute | solution.py:188
  261.3 5.0 %collective-permute-start.10 = (bf16[128,1792]{1,0:T(8,128)(2,1)S(1)}, bf16[128,1792]{1,0:T(8,128)(2,1)S(1)}, u32[]{:S(2)}, u32[]{:S(2)}) collective-permute-start(bf16[128,1792]{1,0:T(8,128)(2,1)S(1)} %get-tuple-element.88), channel_id=1, source_target_pairs={{0,8},{4,12},{8,16},{12,20},{16,24},{20,28},{1,9},{5,13},{9,17},{1... | collective-permute-start | bytes 1376264 | tf_op jit(solution)/shard_map/ppermute | solution.py:188
  266.3 3.9 %collective-permute-done.23 = bf16[128,1792]{1,0:T(8,128)(2,1)S(1)} collective-permute-done((bf16[128,1792]{1,0:T(8,128)(2,1)S(1)}, bf16[128,1792]{1,0:T(8,128)(2,1)S(1)}, u32[]{:S(2)}, u32[]{:S(2)}) %collective-permute-start.23) | collective-permute-done | bytes 458784 | tf_op jit(solution)/shard_map/ppermute | solution.py:188
  271.1 5.0 %collective-permute-start.17 = (bf16[128,1792]{1,0:T(8,128)(2,1)S(1)}, bf16[128,1792]{1,0:T(8,128)(2,1)S(1)}, u32[]{:S(2)}, u32[]{:S(2)}) collective-permute-start(bf16[128,1792]{1,0:T(8,128)(2,1)S(1)} %get-tuple-element.92), channel_id=1, source_target_pairs={{0,8},{4,12},{8,16},{12,20},{16,24},{20,28},{1,9},{5,13},{9,17},{1... | collective-permute-start | bytes 1376264 | tf_op jit(solution)/shard_map/ppermute | solution.py:188
  277.0 12.9 %collective-permute-start.24 = (bf16[128,1792]{1,0:T(8,128)(2,1)S(1)}, bf16[128,1792]{1,0:T(8,128)(2,1)S(1)}, u32[]{:S(2)}, u32[]{:S(2)}) collective-permute-start(bf16[128,1792]{1,0:T(8,128)(2,1)S(1)} %get-tuple-element.105), channel_id=1, source_target_pairs={{0,8},{4,12},{8,16},{12,20},{16,24},{20,28},{1,9},{5,13},{9,17},{1... | collective-permute-start | bytes 1376264 | tf_op jit(solution)/shard_map/ppermute | solution.py:188
  292.7 13.8 %collective-permute-done.6 = bf16[128,1792]{1,0:T(8,128)(2,1)S(1)} collective-permute-done((bf16[128,1792]{1,0:T(8,128)(2,1)S(1)}, bf16[128,1792]{1,0:T(8,128)(2,1)S(1)}, u32[]{:S(2)}, u32[]{:S(2)}) %collective-permute-start.6) | collective-permute-done | bytes 458784 | tf_op jit(solution)/shard_map/ppermute | solution.py:188
  309.4 7.0 %collective-permute-done.13 = bf16[128,1792]{1,0:T(8,128)(2,1)S(1)} collective-permute-done((bf16[128,1792]{1,0:T(8,128)(2,1)S(1)}, bf16[128,1792]{1,0:T(8,128)(2,1)S(1)}, u32[]{:S(2)}, u32[]{:S(2)}) %collective-permute-start.13) | collective-permute-done | bytes 458784 | tf_op jit(solution)/shard_map/ppermute | solution.py:188
  316.5 8.7 %collective-permute-done.20 = bf16[128,1792]{1,0:T(8,128)(2,1)S(1)} collective-permute-done((bf16[128,1792]{1,0:T(8,128)(2,1)S(1)}, bf16[128,1792]{1,0:T(8,128)(2,1)S(1)}, u32[]{:S(2)}, u32[]{:S(2)}) %collective-permute-start.20) | collective-permute-done | bytes 458784 | tf_op jit(solution)/shard_map/ppermute | solution.py:188
  325.6 4.5 %collective-permute-done.27 = bf16[128,1792]{1,0:T(8,128)(2,1)S(1)} collective-permute-done((bf16[128,1792]{1,0:T(8,128)(2,1)S(1)}, bf16[128,1792]{1,0:T(8,128)(2,1)S(1)}, u32[]{:S(2)}, u32[]{:S(2)}) %collective-permute-start.27) | collective-permute-done | bytes 458784 | tf_op jit(solution)/shard_map/ppermute | solution.py:188
  (129 shorter events, 36.9 us)
Async XLA Ops:
  7.2 50.7 %all-gather.4.cloned.1.call-start = ((), (), s32[]{:S(2)}) async-start(), calls=%async_computation.1 | async-start | bytes 1310720 | tf_op jit(solution)/shard_map/all_gather | solution.py:157
  33.9 1.1 copy-start.13
  33.9 1.6 copy-start.14
  40.4 4.5 %copy-start.5 = (bf16[512,896]{1,0:T(8,128)(2,1)}, bf16[512,896]{1,0:T(8,128)(2,1)S(1)}, u32[]{:S(2)}) copy-start(bf16[512,896]{1,0:T(8,128)(2,1)S(1)} %get-tuple-element.71) | copy-start | bytes 2752516
  40.4 4.5 %copy-start.7 = (bf16[512,896]{1,0:T(8,128)(2,1)}, bf16[512,896]{1,0:T(8,128)(2,1)S(1)}, u32[]{:S(2)}) copy-start(bf16[512,896]{1,0:T(8,128)(2,1)S(1)} %get-tuple-element.137) | copy-start | bytes 2752516
  40.4 4.5 %copy-start.9 = (bf16[512,896]{1,0:T(8,128)(2,1)}, bf16[512,896]{1,0:T(8,128)(2,1)S(1)}, u32[]{:S(2)}) copy-start(bf16[512,896]{1,0:T(8,128)(2,1)S(1)} %get-tuple-element.70) | copy-start | bytes 2752516
  40.4 4.5 %copy-start.11 = (bf16[512,896]{1,0:T(8,128)(2,1)}, bf16[512,896]{1,0:T(8,128)(2,1)S(1)}, u32[]{:S(2)}) copy-start(bf16[512,896]{1,0:T(8,128)(2,1)S(1)} %get-tuple-element.138) | copy-start | bytes 2752516
  40.5 5.2 %copy-start.1 = (bf16[512,896]{1,0:T(8,128)(2,1)}, bf16[512,896]{1,0:T(8,128)(2,1)S(1)}, u32[]{:S(2)}) copy-start(bf16[512,896]{1,0:T(8,128)(2,1)S(1)} %get-tuple-element.73) | copy-start | bytes 2752516
  40.5 5.1 %copy-start.3 = (bf16[512,896]{1,0:T(8,128)(2,1)}, bf16[512,896]{1,0:T(8,128)(2,1)S(1)}, u32[]{:S(2)}) copy-start(bf16[512,896]{1,0:T(8,128)(2,1)S(1)} %get-tuple-element.135) | copy-start | bytes 2752516
  42.0 54.1 %collective-permute-start = (bf16[512,1792]{1,0:T(8,128)(2,1)}, bf16[512,1792]{1,0:T(8,128)(2,1)}, u32[]{:S(2)}, u32[]{:S(2)}) collective-permute-start(bf16[512,1792]{1,0:T(8,128)(2,1)} %pad_maximum_fusion), channel_id=1, source_target_pairs={{0,4},{4,0},{8,12},{12,8},{16,20},{20,16},{24,28},{28,24},{1,5},{5... | collective-permute-start | bytes 5505032 | tf_op jit(solution)/shard_map/ppermute | solution.py:111
  44.9 79.6 %collective-permute-start.7 = (bf16[512,1792]{1,0:T(8,128)(2,1)}, bf16[512,1792]{1,0:T(8,128)(2,1)}, u32[]{:S(2)}, u32[]{:S(2)}) collective-permute-start(bf16[512,1792]{1,0:T(8,128)(2,1)} %pad_maximum_fusion.1), channel_id=1, source_target_pairs={{0,4},{4,0},{8,12},{12,8},{16,20},{20,16},{24,28},{28,24},{1,5},{5... | collective-permute-start | bytes 5505032 | tf_op jit(solution)/shard_map/ppermute | solution.py:111
  47.0 116.8 %collective-permute-start.14 = (bf16[512,1792]{1,0:T(8,128)(2,1)}, bf16[512,1792]{1,0:T(8,128)(2,1)}, u32[]{:S(2)}, u32[]{:S(2)}) collective-permute-start(bf16[512,1792]{1,0:T(8,128)(2,1)} %pad_maximum_fusion.2), channel_id=1, source_target_pairs={{0,4},{4,0},{8,12},{12,8},{16,20},{20,16},{24,28},{28,24},{1,5},{5... | collective-permute-start | bytes 5505032 | tf_op jit(solution)/shard_map/ppermute | solution.py:111
  49.8 152.8 %collective-permute-start.21 = (bf16[512,1792]{1,0:T(8,128)(2,1)}, bf16[512,1792]{1,0:T(8,128)(2,1)}, u32[]{:S(2)}, u32[]{:S(2)}) collective-permute-start(bf16[512,1792]{1,0:T(8,128)(2,1)} %pad_maximum_fusion.3), channel_id=1, source_target_pairs={{0,4},{4,0},{8,12},{12,8},{16,20},{20,16},{24,28},{28,24},{1,5},{5... | collective-permute-start | bytes 5505032 | tf_op jit(solution)/shard_map/ppermute | solution.py:111
  60.2 30.4 %all-to-all-start = ((bf16[4,128,1024]{2,1,0:T(8,128)(2,1)}), bf16[4,128,1024]{2,1,0:T(8,128)(2,1)}, u32[]{:S(2)}, u32[]{:S(2)}) async-start(bf16[4,128,1024]{2,1,0:T(8,128)(2,1)} %bitcast.231), calls=%async_computation | async-start | bytes 2097152 | tf_op jit(solution)/shard_map/all_to_all | solution.py:162
  65.1 5.8 %copy-start = (f32[4,1024,512]{1,2,0:T(8,128)S(1)}, f32[4,1024,512]{1,2,0:T(8,128)}, u32[]{:S(2)}) copy-start(f32[4,1024,512]{1,2,0:T(8,128)} %get-tuple-element.128) | copy-start | bytes 25165828
  92.5 2.5 copy-start.10
  92.5 2.5 copy-start.12
  96.1 4.9 %copy-start.6 = (bf16[512,896]{1,0:T(8,128)(2,1)S(1)}, bf16[512,896]{1,0:T(8,128)(2,1)}, u32[]{:S(2)}) copy-start(bf16[512,896]{1,0:T(8,128)(2,1)} %copy-done.5) | copy-start | bytes 2752516
  96.1 4.9 %copy-start.8 = (bf16[512,896]{1,0:T(8,128)(2,1)S(1)}, bf16[512,896]{1,0:T(8,128)(2,1)}, u32[]{:S(2)}) copy-start(bf16[512,896]{1,0:T(8,128)(2,1)} %copy-done.7) | copy-start | bytes 2752516
  99.0 109.9 %collective-permute-start.1 = (bf16[128,1792]{1,0:T(8,128)(2,1)S(1)}, bf16[128,1792]{1,0:T(8,128)(2,1)S(1)}, u32[]{:S(2)}, u32[]{:S(2)}) collective-permute-start(bf16[128,1792]{1,0:T(8,128)(2,1)S(1)} %get-tuple-element.68), channel_id=1, source_target_pairs={{0,8},{4,12},{1,9},{5,13},{2,10},{6,14},{3,11},{7,15}} | collective-permute-start | bytes 1376264 | tf_op jit(solution)/shard_map/ppermute | solution.py:188
  100.3 129.6 %collective-permute-start.4 = (bf16[128,1792]{1,0:T(8,128)(2,1)S(1)}, bf16[128,1792]{1,0:T(8,128)(2,1)S(1)}, u32[]{:S(2)}, u32[]{:S(2)}) collective-permute-start(bf16[128,1792]{1,0:T(8,128)(2,1)S(1)} %get-tuple-element.69), channel_id=1, source_target_pairs={{24,16},{28,20},{25,17},{29,21},{26,18},{30,22},{27,19},{31,23}} | collective-permute-start | bytes 1376264 | tf_op jit(solution)/shard_map/ppermute | solution.py:188
  102.1 28.7 %copy-start.2 = (bf16[512,896]{1,0:T(8,128)(2,1)S(1)}, bf16[512,896]{1,0:T(8,128)(2,1)}, u32[]{:S(2)}) copy-start(bf16[512,896]{1,0:T(8,128)(2,1)} %copy-done.1) | copy-start | bytes 2752516
  102.1 28.7 %copy-start.4 = (bf16[512,896]{1,0:T(8,128)(2,1)S(1)}, bf16[512,896]{1,0:T(8,128)(2,1)}, u32[]{:S(2)}) copy-start(bf16[512,896]{1,0:T(8,128)(2,1)} %copy-done.3) | copy-start | bytes 2752516
  127.2 82.4 %collective-permute-start.8 = (bf16[128,1792]{1,0:T(8,128)(2,1)S(1)}, bf16[128,1792]{1,0:T(8,128)(2,1)S(1)}, u32[]{:S(2)}, u32[]{:S(2)}) collective-permute-start(bf16[128,1792]{1,0:T(8,128)(2,1)S(1)} %get-tuple-element.90), channel_id=1, source_target_pairs={{0,8},{4,12},{1,9},{5,13},{2,10},{6,14},{3,11},{7,15}} | collective-permute-start | bytes 1376264 | tf_op jit(solution)/shard_map/ppermute | solution.py:188
  163.8 81.5 %collective-permute-start.11 = (bf16[128,1792]{1,0:T(8,128)(2,1)S(1)}, bf16[128,1792]{1,0:T(8,128)(2,1)S(1)}, u32[]{:S(2)}, u32[]{:S(2)}) collective-permute-start(bf16[128,1792]{1,0:T(8,128)(2,1)S(1)} %get-tuple-element.91), channel_id=1, source_target_pairs={{24,16},{28,20},{25,17},{29,21},{26,18},{30,22},{27,19},{31,23}} | collective-permute-start | bytes 1376264 | tf_op jit(solution)/shard_map/ppermute | solution.py:188
  202.6 14.5 %collective-permute-start.15 = (bf16[128,1792]{1,0:T(8,128)(2,1)S(1)}, bf16[128,1792]{1,0:T(8,128)(2,1)S(1)}, u32[]{:S(2)}, u32[]{:S(2)}) collective-permute-start(bf16[128,1792]{1,0:T(8,128)(2,1)S(1)} %get-tuple-element.103), channel_id=1, source_target_pairs={{0,8},{4,12},{1,9},{5,13},{2,10},{6,14},{3,11},{7,15}} | collective-permute-start | bytes 1376264 | tf_op jit(solution)/shard_map/ppermute | solution.py:188
  208.9 42.5 %collective-permute-start.18 = (bf16[128,1792]{1,0:T(8,128)(2,1)S(1)}, bf16[128,1792]{1,0:T(8,128)(2,1)S(1)}, u32[]{:S(2)}, u32[]{:S(2)}) collective-permute-start(bf16[128,1792]{1,0:T(8,128)(2,1)S(1)} %get-tuple-element.104), channel_id=1, source_target_pairs={{24,16},{28,20},{25,17},{29,21},{26,18},{30,22},{27,19},{31,23}} | collective-permute-start | bytes 1376264 | tf_op jit(solution)/shard_map/ppermute | solution.py:188
  209.7 15.7 %collective-permute-start.22 = (bf16[128,1792]{1,0:T(8,128)(2,1)S(1)}, bf16[128,1792]{1,0:T(8,128)(2,1)S(1)}, u32[]{:S(2)}, u32[]{:S(2)}) collective-permute-start(bf16[128,1792]{1,0:T(8,128)(2,1)S(1)} %get-tuple-element.107), channel_id=1, source_target_pairs={{0,8},{4,12},{1,9},{5,13},{2,10},{6,14},{3,11},{7,15}} | collective-permute-start | bytes 1376264 | tf_op jit(solution)/shard_map/ppermute | solution.py:188
  217.0 44.2 %collective-permute-start.25 = (bf16[128,1792]{1,0:T(8,128)(2,1)S(1)}, bf16[128,1792]{1,0:T(8,128)(2,1)S(1)}, u32[]{:S(2)}, u32[]{:S(2)}) collective-permute-start(bf16[128,1792]{1,0:T(8,128)(2,1)S(1)} %get-tuple-element.108), channel_id=1, source_target_pairs={{24,16},{28,20},{25,17},{29,21},{26,18},{30,22},{27,19},{31,23}} | collective-permute-start | bytes 1376264 | tf_op jit(solution)/shard_map/ppermute | solution.py:188
  225.4 15.3 %collective-permute-start.2 = (bf16[128,1792]{1,0:T(8,128)(2,1)S(1)}, bf16[128,1792]{1,0:T(8,128)(2,1)S(1)}, u32[]{:S(2)}, u32[]{:S(2)}) collective-permute-start(bf16[128,1792]{1,0:T(8,128)(2,1)S(1)} %fusion.37), channel_id=1, source_target_pairs={{0,8},{4,12},{8,16},{12,20},{1,9},{5,13},{9,17},{13,21},{2,10},{6,... | collective-permute-start | bytes 1376264 | tf_op jit(solution)/shard_map/ppermute | solution.py:188
  229.9 20.7 %collective-permute-start.9 = (bf16[128,1792]{1,0:T(8,128)(2,1)S(1)}, bf16[128,1792]{1,0:T(8,128)(2,1)S(1)}, u32[]{:S(2)}, u32[]{:S(2)}) collective-permute-start(bf16[128,1792]{1,0:T(8,128)(2,1)S(1)} %fusion.32), channel_id=1, source_target_pairs={{0,8},{4,12},{8,16},{12,20},{1,9},{5,13},{9,17},{13,21},{2,10},{6,... | collective-permute-start | bytes 1376264 | tf_op jit(solution)/shard_map/ppermute | solution.py:188
  240.7 19.7 %collective-permute-start.16 = (bf16[128,1792]{1,0:T(8,128)(2,1)S(1)}, bf16[128,1792]{1,0:T(8,128)(2,1)S(1)}, u32[]{:S(2)}, u32[]{:S(2)}) collective-permute-start(bf16[128,1792]{1,0:T(8,128)(2,1)S(1)} %fusion.27), channel_id=1, source_target_pairs={{0,8},{4,12},{8,16},{12,20},{1,9},{5,13},{9,17},{13,21},{2,10},{6,... | collective-permute-start | bytes 1376264 | tf_op jit(solution)/shard_map/ppermute | solution.py:188
  245.3 24.9 %collective-permute-start.23 = (bf16[128,1792]{1,0:T(8,128)(2,1)S(1)}, bf16[128,1792]{1,0:T(8,128)(2,1)S(1)}, u32[]{:S(2)}, u32[]{:S(2)}) collective-permute-start(bf16[128,1792]{1,0:T(8,128)(2,1)S(1)} %fusion.22), channel_id=1, source_target_pairs={{0,8},{4,12},{8,16},{12,20},{1,9},{5,13},{9,17},{13,21},{2,10},{6,... | collective-permute-start | bytes 1376264 | tf_op jit(solution)/shard_map/ppermute | solution.py:188
  250.6 20.5 %collective-permute-start.5 = (bf16[128,1792]{1,0:T(8,128)(2,1)S(1)}, bf16[128,1792]{1,0:T(8,128)(2,1)S(1)}, u32[]{:S(2)}, u32[]{:S(2)}) collective-permute-start(bf16[128,1792]{1,0:T(8,128)(2,1)S(1)} %get-tuple-element.67), channel_id=1, source_target_pairs={{16,8},{20,12},{24,16},{28,20},{17,9},{21,13},{25,17},{29,21},{18,... | collective-permute-start | bytes 1376264 | tf_op jit(solution)/shard_map/ppermute | solution.py:188
  251.4 40.0 %collective-permute-start.3 = (bf16[128,1792]{1,0:T(8,128)(2,1)S(1)}, bf16[128,1792]{1,0:T(8,128)(2,1)S(1)}, u32[]{:S(2)}, u32[]{:S(2)}) collective-permute-start(bf16[128,1792]{1,0:T(8,128)(2,1)S(1)} %get-tuple-element.66), channel_id=1, source_target_pairs={{0,8},{4,12},{8,16},{12,20},{16,24},{20,28},{1,9},{5,13},{9,17},{1... | collective-permute-start | bytes 1376264 | tf_op jit(solution)/shard_map/ppermute | solution.py:188
  260.4 15.8 %collective-permute-start.12 = (bf16[128,1792]{1,0:T(8,128)(2,1)S(1)}, bf16[128,1792]{1,0:T(8,128)(2,1)S(1)}, u32[]{:S(2)}, u32[]{:S(2)}) collective-permute-start(bf16[128,1792]{1,0:T(8,128)(2,1)S(1)} %get-tuple-element.89), channel_id=1, source_target_pairs={{16,8},{20,12},{24,16},{28,20},{17,9},{21,13},{25,17},{29,21},{18,... | collective-permute-start | bytes 1376264 | tf_op jit(solution)/shard_map/ppermute | solution.py:188
  261.3 46.9 %collective-permute-start.10 = (bf16[128,1792]{1,0:T(8,128)(2,1)S(1)}, bf16[128,1792]{1,0:T(8,128)(2,1)S(1)}, u32[]{:S(2)}, u32[]{:S(2)}) collective-permute-start(bf16[128,1792]{1,0:T(8,128)(2,1)S(1)} %get-tuple-element.88), channel_id=1, source_target_pairs={{0,8},{4,12},{8,16},{12,20},{16,24},{20,28},{1,9},{5,13},{9,17},{1... | collective-permute-start | bytes 1376264 | tf_op jit(solution)/shard_map/ppermute | solution.py:188
  270.2 6.8 %collective-permute-start.19 = (bf16[128,1792]{1,0:T(8,128)(2,1)S(1)}, bf16[128,1792]{1,0:T(8,128)(2,1)S(1)}, u32[]{:S(2)}, u32[]{:S(2)}) collective-permute-start(bf16[128,1792]{1,0:T(8,128)(2,1)S(1)} %get-tuple-element.102), channel_id=1, source_target_pairs={{16,8},{20,12},{24,16},{28,20},{17,9},{21,13},{25,17},{29,21},{18,... | collective-permute-start | bytes 1376264 | tf_op jit(solution)/shard_map/ppermute | solution.py:188
  271.1 45.4 %collective-permute-start.17 = (bf16[128,1792]{1,0:T(8,128)(2,1)S(1)}, bf16[128,1792]{1,0:T(8,128)(2,1)S(1)}, u32[]{:S(2)}, u32[]{:S(2)}) collective-permute-start(bf16[128,1792]{1,0:T(8,128)(2,1)S(1)} %get-tuple-element.92), channel_id=1, source_target_pairs={{0,8},{4,12},{8,16},{12,20},{16,24},{20,28},{1,9},{5,13},{9,17},{1... | collective-permute-start | bytes 1376264 | tf_op jit(solution)/shard_map/ppermute | solution.py:188
  276.2 13.8 %collective-permute-start.26 = (bf16[128,1792]{1,0:T(8,128)(2,1)S(1)}, bf16[128,1792]{1,0:T(8,128)(2,1)S(1)}, u32[]{:S(2)}, u32[]{:S(2)}) collective-permute-start(bf16[128,1792]{1,0:T(8,128)(2,1)S(1)} %get-tuple-element.106), channel_id=1, source_target_pairs={{16,8},{20,12},{24,16},{28,20},{17,9},{21,13},{25,17},{29,21},{18,... | collective-permute-start | bytes 1376264 | tf_op jit(solution)/shard_map/ppermute | solution.py:188
  277.0 48.6 %collective-permute-start.24 = (bf16[128,1792]{1,0:T(8,128)(2,1)S(1)}, bf16[128,1792]{1,0:T(8,128)(2,1)S(1)}, u32[]{:S(2)}, u32[]{:S(2)}) collective-permute-start(bf16[128,1792]{1,0:T(8,128)(2,1)S(1)} %get-tuple-element.105), channel_id=1, source_target_pairs={{0,8},{4,12},{8,16},{12,20},{16,24},{20,28},{1,9},{5,13},{9,17},{1... | collective-permute-start | bytes 1376264 | tf_op jit(solution)/shard_map/ppermute | solution.py:188
  290.0 16.5 %collective-permute-start.6 = (bf16[128,1792]{1,0:T(8,128)(2,1)S(1)}, bf16[128,1792]{1,0:T(8,128)(2,1)S(1)}, u32[]{:S(2)}, u32[]{:S(2)}) collective-permute-start(bf16[128,1792]{1,0:T(8,128)(2,1)S(1)} %fusion.36), channel_id=1, source_target_pairs={{8,0},{12,4},{16,8},{20,12},{24,16},{28,20},{9,1},{13,5},{17,9},{2... | collective-permute-start | bytes 1376264 | tf_op jit(solution)/shard_map/ppermute | solution.py:188
  291.4 25.0 %collective-permute-start.13 = (bf16[128,1792]{1,0:T(8,128)(2,1)S(1)}, bf16[128,1792]{1,0:T(8,128)(2,1)S(1)}, u32[]{:S(2)}, u32[]{:S(2)}) collective-permute-start(bf16[128,1792]{1,0:T(8,128)(2,1)S(1)} %fusion.31), channel_id=1, source_target_pairs={{8,0},{12,4},{16,8},{20,12},{24,16},{28,20},{9,1},{13,5},{17,9},{2... | collective-permute-start | bytes 1376264 | tf_op jit(solution)/shard_map/ppermute | solution.py:188
  306.5 18.6 %collective-permute-start.20 = (bf16[128,1792]{1,0:T(8,128)(2,1)S(1)}, bf16[128,1792]{1,0:T(8,128)(2,1)S(1)}, u32[]{:S(2)}, u32[]{:S(2)}) collective-permute-start(bf16[128,1792]{1,0:T(8,128)(2,1)S(1)} %fusion.26), channel_id=1, source_target_pairs={{8,0},{12,4},{16,8},{20,12},{24,16},{28,20},{9,1},{13,5},{17,9},{2... | collective-permute-start | bytes 1376264 | tf_op jit(solution)/shard_map/ppermute | solution.py:188
  308.1 22.0 %collective-permute-start.27 = (bf16[128,1792]{1,0:T(8,128)(2,1)S(1)}, bf16[128,1792]{1,0:T(8,128)(2,1)S(1)}, u32[]{:S(2)}, u32[]{:S(2)}) collective-permute-start(bf16[128,1792]{1,0:T(8,128)(2,1)S(1)} %fusion.21), channel_id=1, source_target_pairs={{8,0},{12,4},{16,8},{20,12},{24,16},{28,20},{9,1},{13,5},{17,9},{2... | collective-permute-start | bytes 1376264 | tf_op jit(solution)/shard_map/ppermute | solution.py:188
Sparse Core Ops, SparseCore 0:
  36.6 17.6 all-gather.3

commit v2 on v1

--- a/solution.py
+++ b/solution.py
@@ -108,7 +108,9 @@
         )
         for i in range(parts)
     ]
-    others = [lax.ppermute(block, "dp", pair) for block in mine] if inner > 1 else None
+    key_values = jnp.concatenate([prompt_k[0], prompt_v[0]], 1)
+    key_values, mine = lax.optimization_barrier((key_values, mine))
+    others = [lax.ppermute(block, "dp", pair) for block in mine[:2]]
     ptok = prompt_q.shape[1]
     rtok = resp_q.shape[1]
     here = lax.axis_index("ctx")
@@ -139,10 +141,7 @@
         )
 
     resp_state = absorb(fresh_state(rtok), resp_heads, resp_k[0], resp_v[0], 0, own_visible)
-    pieces = (
-        lax.all_gather(prompt_k[0], "ctx", axis=0, tiled=True),
-        lax.all_gather(prompt_v[0], "ctx", axis=0, tiled=True),
-    )
+    pieces = jnp.split(lax.all_gather(key_values, "ctx", axis=0, tiled=True), 2, 1)
     prompt_state = absorb(
         fresh_state(ptok), prompt_heads, pieces[0], pieces[1], jnp.int32(0), prompt_visible
     )
@@ -163,30 +162,56 @@
     columns = columns.reshape(outer * rows, inner, depth)
     own_columns = lax.dynamic_index_in_dim(columns, x, 1, keepdims=False)
     other_columns = lax.dynamic_index_in_dim(columns, (x + 1) % inner, 1, keepdims=False)
-    hidden_parts = []
-    for i in range(parts):
+
+    def partial_products(i):
         partial = jnp.dot(own_columns, mine[i], preferred_element_type=jnp.float32)
         if inner > 1:
             partial = partial + jnp.dot(
                 other_columns, others[i], preferred_element_type=jnp.float32
             )
-        partial = partial.reshape(outer, rows, 2 * part)
-        result = lax.dynamic_index_in_dim(partial, z, 0, keepdims=False)
-        for way in (1, -1):
-            arrived = jnp.zeros((rows, 2 * part), jnp.float32)
-            for step in range(outer - 1):
-                target = jnp.clip(z + way * (outer - 1 - step), 0, outer - 1)
-                term = lax.dynamic_index_in_dim(partial, target, 0, keepdims=False)
-                perm = []
-                for source in range(outer):
-                    rank = source if way == 1 else outer - 1 - source
-                    if rank <= step:
-                        perm += [
-                            (source * inner + j, (source + way) * inner + j) for j in range(inner)
-                        ]
-                sent = (term + arrived).astype(jnp.bfloat16)
-                arrived = lax.ppermute(sent, "dp", perm).astype(jnp.float32)
-            result = result + arrived
+        return partial.reshape(outer, rows, 2 * part)
+
+    steps = outer - 1
+
+    def advance(partial, arrived, step):
+        result = []
+        for way, before in zip((1, -1), arrived):
+            target = jnp.clip(z + way * (steps - step), 0, outer - 1)
+            sent = lax.dynamic_index_in_dim(partial, target, 0, keepdims=False)
+            if before is not None:
+                sent = sent + before.astype(jnp.float32)
+            perm = []
+            for source in range(outer):
+                rank = source if way == 1 else outer - 1 - source
+                if rank <= step:
+                    perm += [
+                        (source * inner + j, (source + way) * inner + j) for j in range(inner)
+                    ]
+            result.append(lax.ppermute(sent.astype(jnp.bfloat16), "dp", perm))
+        return tuple(result)
+
+    partials = [None] * parts
+    flows = [[(None, None)] for _ in range(parts)]
+    hidden_parts = []
+    for turn in range(parts + steps):
+        if turn < parts:
+            if 1 <= turn < parts - 1:
+                behind = range(max(turn - 2, 0), turn)
+                waited = [flows[i][-1] for i in behind]
+                block, waited = lax.optimization_barrier((mine[turn + 1], waited))
+                for i, arrived in zip(behind, waited):
+                    flows[i][-1] = arrived
+                others.append(lax.ppermute(block, "dp", pair))
+            partials[turn] = partial_products(turn)
+        for i in range(parts):
+            step = turn - i
+            if 0 <= step < steps:
+                flows[i].append(advance(partials[i], flows[i][-1], step))
+    for i in range(parts):
+        result = lax.dynamic_index_in_dim(partials[i], z, 0, keepdims=False)
+        for arrived in flows[i][-1]:
+            if arrived is not None:
+                result = result + arrived.astype(jnp.float32)
         gate, up = result[:, :part], result[:, part:]
         hidden_parts.append((jax.nn.silu(gate) * up).astype(jnp.bfloat16))
     hidden = jnp.concatenate(hidden_parts, 1)

time: 339 us -> 307 us (0.906)
  waiting for transfers between devices: 167 us -> 148 us
  blocking collectives: 16 us -> 0 us
    ppermute x28, waiting for transfers between devices: 156 us -> 112 us  [the longest x24 55.5 us: advance(): result.append(lax.ppermute(sent.astype(jnp.bfloat16), 'dp', perm))]
    all_gather x0 -> x1, waiting for transfers between devices: none -> 16.4 us  [local(): lax.all_gather(key_values, 'ctx', axis=0, tiled=True)]
    all_gather x2 -> x0, blocking collectives: 16 us -> none  [the longest x1 8.65 us: local(): lax.all_gather(prompt_k[0], 'ctx', axis=0, tiled=True)]
    all_gather x1, waiting for transfers between devices: 0.02 us -> 5.11 us  [local(): grouped_rows = lax.all_gather(normed, 'ctx', axis=0, tiled=True)]
  transfers between devices with their start and end apart: 30 -> 31, of which waited for: 14 -> 18; matrix products, arithmetic and copies ran while one was open for 16% -> 15% of each run, Pallas kernels for 0% -> 0%
where the time goes in v2:
time: 307 us; the launch traced here: 304 us
  waiting for transfers between devices  148 us (48%)
  starting transfers between devices  73 us (24%)
  local copies, waits for them, and re-layouts  25.1 us (8%)
  matrix products  24.3 us (8%)
  other arithmetic  18.5 us (6%)
  between operations  15.5 us (5%)
    ppermute x24, starting transfers between devices, advance(): result.append(lax.ppermute(sent.astype(jnp.bfloat16), 'dp', perm))  63.1 us
    ppermute x24, waiting for transfers between devices, advance(): result.append(lax.ppermute(sent.astype(jnp.bfloat16), 'dp', perm))  55.5 us
    ppermute x2, waiting for transfers between devices, local(): others.append(lax.ppermute(block, 'dp', pair))  30.1 us
    ppermute x2, waiting for transfers between devices, local(): others = [lax.ppermute(block, 'dp', pair) for block in mine[:2]]  26.4 us
    all_gather x1, waiting for transfers between devices, local(): lax.all_gather(key_values, 'ctx', axis=0, tiled=True)  16.4 us
    all_to_all x1, waiting for transfers between devices, local(): lax.all_to_all(columns, 'dp', 0, 0, axis_index_groups=groups, tiled=True)  14.3 us
    dot_general x4, matrix products, partial_products(): jnp.dot(other_columns, others[i], preferred_element_type=jnp.float32)  7.49 us
    dot_general x3, matrix products, one_block(): jnp.einsum('kqd,ktd->kqt', queries, key_matrix, preferred_element_type=jn...  6.83 us
  transfers between devices with their start and end apart: 31, of which 18 were waited for; matrix products, arithmetic and copies ran while one was open for 15% of the time, Pallas kernels for 0%

profile of v2, /device:TPU:0, one launch (start us, length us, event | category | flops | bytes accessed | tf_op | source)
XLA Modules:
  0.0 304.1 jit_solution(1192508317999872924)
XLA Ops:
  7.2 3.8 %fusion.93 = (bf16[512,896]{1,0:T(8,128)(2,1)}, bf16[512,896]{1,0:T(8,128)(2,1)S(1)}, bf16[512,896]{1,0:T(8,128)(2,1)}, bf16[512,896]{1,0:T(8,128)(2,1)}) fusion(bf16[512,3584]{1,0:T(8,128)(2,1)} %param.22), kind=kLoop, calls=%fused_computation.165 | loop fusion | bytes 7340032 | tf_op jit(solution)/shard_map/slice | solution.py:107
  11.0 1.9 fusion.94
  13.9 3.7 %pad_maximum_fusion.2 = (bf16[512,1792]{1,0:T(8,128)(2,1)}, bf16[512,1792]{1,0:T(8,128)(2,1)S(1)}) fusion(bf16[512,896]{1,0:T(8,128)(2,1)} %get-tuple-element.145, bf16[512,896]{1,0:T(8,128)(2,1)} %get-tuple-element.141, bf16[512,896]{1,0:T(8,128)(2,1)} %get-tuple-element.142, bf16[512,896]{1,0:T(8,128)(2,1)} %get-tuple-element.138), kind=kLoop, calls=%fused_computation.20 | loop fusion | flops 7340032 | bytes 7340032 | tf_op jit(solution)/shard_map/concatenate | solution.py:106
  17.6 2.1 pad_maximum_fusion
  23.1 16.4 %all-gather.3.cloned.1.call-done = bf16[512,1024]{0,1:T(8,128)(2,1)} async-done(((bf16[128,1024]{0,1:T(8,128)(2,1)}), bf16[512,1024]{0,1:T(8,128)(2,1)}) %all-gather.3.cloned.1.call-update) | async-done | bytes 1048592 | tf_op jit(solution)/shard_map/all_gather | solution.py:144
  39.5 2.1 fusion.95
  41.6 1.3 copy.24
  48.4 1.5 collective-permute-start.5
  51.2 1.4 copy.41
  52.6 1.4 copy.25
  54.0 6.2 %fusion = (f32[4,1024]{1,0:T(4,128)S(1)}, f32[4,512,1024]{2,1,0:T(8,128)}) fusion(pred[1024,512]{0,1:T(8,128)(4,1)S(1)} %bitcast.255, bf16[4,1024,128]{2,1,0:T(8,128)(2,1)} %bitcast.260, bf16[512,4,128]{2,0,1:T(8,128)(2,1)S(1)} %copy.24), kind=kOutput, calls=%fused_computation.2 | convolution fusion | flops 543158272 | bytes 10502144 | tf_op jit(solution)/shard_map/while/body/eval_jaxpr/kqd,ktd->kqt/dot_general | solution.py:61
  60.2 5.1 %all-gather.5.cloned.1.call-done = bf16[128,4096]{1,0:T(8,128)(2,1)} async-done(((bf16[32,4096]{1,0:T(8,128)(2,1)}), bf16[128,4096]{1,0:T(8,128)(2,1)}) %all-gather.5.cloned.1.call-update) | async-done | bytes 1048592 | tf_op jit(solution)/shard_map/all_gather | solution.py:156
  65.3 2.3 copy.62
  67.6 4.6 %all-to-all-start = ((bf16[4,128,1024]{2,1,0:T(8,128)(2,1)}), bf16[4,128,1024]{2,1,0:T(8,128)(2,1)}, u32[]{:S(2)}, u32[]{:S(2)}) async-start(bf16[4,128,1024]{2,1,0:T(8,128)(2,1)} %bitcast.261), calls=%async_computation | async-start | bytes 2097152 | tf_op jit(solution)/shard_map/all_to_all | solution.py:161
  72.2 4.7 %fusion.1 = f32[4,1024]{1,0:T(4,128)S(1)} fusion(f32[4,512,1024]{2,1,0:T(8,128)} %get-tuple-element.158, f32[4,1024]{1,0:T(4,128)S(1)} %broadcast_maximum_fusion, pred[1024,512]{0,1:T(8,128)(4,1)S(1)} %bitcast.256), kind=kLoop, calls=%fused_computation.3 | loop fusion | flops 10481664 | bytes 8945664 | tf_op jit(solution)/shard_map/while/body/eval_jaxpr/reduce_sum | solution.py:68
  78.0 4.1 %divide_convert_fusion = bf16[4,1024,128]{2,1,0:T(8,128)(2,1)S(1)} fusion(f32[4,512,1024]{2,1,0:T(8,128)S(1)} %copy-done, f32[4,1024]{1,0:T(4,128)S(1)} %broadcast_maximum_fusion, pred[1024,512]{0,1:T(8,128)(4,1)S(1)} %bitcast.257, f32[4,1024]{1,0:T(4,128)S(1)} %get-tuple-element.151, f32[4,1024]{1,0:T(4,128)S(1)} %get-tuple-element.150, ...), kind=kOutput, calls=%fused_computation.16 | convolution fusion | flops 548929536 | bytes 10534912 | tf_op jit(solution)/shard_map/while/body/eval_jaxpr/kqt,ktd->kqd/dot_general | solution.py:69
  84.1 14.3 %all-to-all-done = bf16[4,128,1024]{2,1,0:T(8,128)(2,1)} async-done(((bf16[4,128,1024]{2,1,0:T(8,128)(2,1)}), bf16[4,128,1024]{2,1,0:T(8,128)(2,1)}, u32[]{:S(2)}, u32[]{:S(2)}) %all-to-all-start) | async-done | bytes 1048608 | tf_op jit(solution)/shard_map/all_to_all | solution.py:161
  98.4 1.8 reshape.321
  100.2 2.2 constant_dynamic-slice_fusion
  103.8 26.4 %collective-permute-done = bf16[512,1792]{1,0:T(8,128)(2,1)} collective-permute-done((bf16[512,1792]{1,0:T(8,128)(2,1)}, bf16[512,1792]{1,0:T(8,128)(2,1)}, u32[]{:S(2)}, u32[]{:S(2)}) %collective-permute-start) | collective-permute-done | bytes 1835040 | tf_op jit(solution)/shard_map/ppermute | solution.py:113
  130.3 2.6 convolution_add_fusion.3
  133.0 3.4 %collective-permute-start.1 = (bf16[128,1792]{1,0:T(8,128)(2,1)S(1)}, bf16[128,1792]{1,0:T(8,128)(2,1)S(1)}, u32[]{:S(2)}, u32[]{:S(2)}) collective-permute-start(bf16[128,1792]{1,0:T(8,128)(2,1)S(1)} %get-tuple-element.137), channel_id=1, source_target_pairs={{0,8},{4,12},{1,9},{5,13},{2,10},{6,14},{3,11},{7,15}} | collective-permute-start | bytes 1376264 | tf_op jit(solution)/shard_map/ppermute | solution.py:190
  138.3 2.6 convolution_add_fusion.2
  141.0 1.4 collective-permute-start.6
  143.2 4.2 %collective-permute-done.1 = bf16[128,1792]{1,0:T(8,128)(2,1)S(1)} collective-permute-done((bf16[128,1792]{1,0:T(8,128)(2,1)S(1)}, bf16[128,1792]{1,0:T(8,128)(2,1)S(1)}, u32[]{:S(2)}, u32[]{:S(2)}) %collective-permute-start.1) | collective-permute-done | bytes 458784 | tf_op jit(solution)/shard_map/ppermute | solution.py:190
  147.5 4.4 %collective-permute-start.3 = (bf16[128,1792]{1,0:T(8,128)(2,1)S(1)}, bf16[128,1792]{1,0:T(8,128)(2,1)S(1)}, u32[]{:S(2)}, u32[]{:S(2)}) collective-permute-start(bf16[128,1792]{1,0:T(8,128)(2,1)S(1)} %get-tuple-element.135), channel_id=1, source_target_pairs={{0,8},{4,12},{8,16},{12,20},{1,9},{5,13},{9,17},{13,21},{2,10},{6,... | collective-permute-start | bytes 1376264 | tf_op jit(solution)/shard_map/ppermute | solution.py:190
  155.1 1.5 collective-permute-start.14
  157.2 8.2 %collective-permute-done.3 = bf16[128,1792]{1,0:T(8,128)(2,1)S(1)} collective-permute-done((bf16[128,1792]{1,0:T(8,128)(2,1)S(1)}, bf16[128,1792]{1,0:T(8,128)(2,1)S(1)}, u32[]{:S(2)}, u32[]{:S(2)}) %collective-permute-start.3) | collective-permute-done | bytes 458784 | tf_op jit(solution)/shard_map/ppermute | solution.py:190
  165.5 4.4 %collective-permute-start.10 = (bf16[128,1792]{1,0:T(8,128)(2,1)S(1)}, bf16[128,1792]{1,0:T(8,128)(2,1)S(1)}, u32[]{:S(2)}, u32[]{:S(2)}) collective-permute-start(bf16[128,1792]{1,0:T(8,128)(2,1)S(1)} %fusion.34), channel_id=1, source_target_pairs={{0,8},{4,12},{8,16},{12,20},{1,9},{5,13},{9,17},{13,21},{2,10},{6,... | collective-permute-start | bytes 1376264 | tf_op jit(solution)/shard_map/ppermute | solution.py:190
  170.1 4.1 %collective-permute-start.8 = (bf16[128,1792]{1,0:T(8,128)(2,1)S(1)}, bf16[128,1792]{1,0:T(8,128)(2,1)S(1)}, u32[]{:S(2)}, u32[]{:S(2)}) collective-permute-start(bf16[128,1792]{1,0:T(8,128)(2,1)S(1)} %get-tuple-element.120), channel_id=1, source_target_pairs={{0,8},{4,12},{8,16},{12,20},{16,24},{20,28},{1,9},{5,13},{9,17},{1... | collective-permute-start | bytes 1376264 | tf_op jit(solution)/shard_map/ppermute | solution.py:190
  175.5 1.6 collective-permute-start.21
  177.0 3.8 %collective-permute-done.10 = bf16[128,1792]{1,0:T(8,128)(2,1)S(1)} collective-permute-done((bf16[128,1792]{1,0:T(8,128)(2,1)S(1)}, bf16[128,1792]{1,0:T(8,128)(2,1)S(1)}, u32[]{:S(2)}, u32[]{:S(2)}) %collective-permute-start.10) | collective-permute-done | bytes 458784 | tf_op jit(solution)/shard_map/ppermute | solution.py:190
  181.7 6.4 %collective-permute-done.8 = bf16[128,1792]{1,0:T(8,128)(2,1)S(1)} collective-permute-done((bf16[128,1792]{1,0:T(8,128)(2,1)S(1)}, bf16[128,1792]{1,0:T(8,128)(2,1)S(1)}, u32[]{:S(2)}, u32[]{:S(2)}) %collective-permute-start.8) | collective-permute-done | bytes 458784 | tf_op jit(solution)/shard_map/ppermute | solution.py:190
  188.1 4.4 %collective-permute-start.11 = (bf16[128,1792]{1,0:T(8,128)(2,1)S(1)}, bf16[128,1792]{1,0:T(8,128)(2,1)S(1)}, u32[]{:S(2)}, u32[]{:S(2)}) collective-permute-start(bf16[128,1792]{1,0:T(8,128)(2,1)S(1)} %get-tuple-element.122), channel_id=1, source_target_pairs={{0,8},{4,12},{8,16},{12,20},{16,24},{20,28},{1,9},{5,13},{9,17},{1... | collective-permute-start | bytes 1376264 | tf_op jit(solution)/shard_map/ppermute | solution.py:190
  194.3 3.9 %collective-permute-done.14 = bf16[512,1792]{1,0:T(8,128)(2,1)S(1)} collective-permute-done((bf16[512,1792]{1,0:T(8,128)(2,1)S(1)}, bf16[512,1792]{1,0:T(8,128)(2,1)S(1)}, u32[]{:S(2)}, u32[]{:S(2)}) %collective-permute-start.14) | collective-permute-done | bytes 1835040 | tf_op jit(solution)/shard_map/ppermute | solution.py:204
  199.4 4.7 %collective-permute-start.15 = (bf16[128,1792]{1,0:T(8,128)(2,1)S(1)}, bf16[128,1792]{1,0:T(8,128)(2,1)S(1)}, u32[]{:S(2)}, u32[]{:S(2)}) collective-permute-start(bf16[128,1792]{1,0:T(8,128)(2,1)S(1)} %get-tuple-element.126), channel_id=1, source_target_pairs={{0,8},{4,12},{1,9},{5,13},{2,10},{6,14},{3,11},{7,15}} | collective-permute-start | bytes 1376264 | tf_op jit(solution)/shard_map/ppermute | solution.py:190
  204.8 1.7 collective-permute-done.13
  206.8 26.2 %collective-permute-done.21 = bf16[512,1792]{1,0:T(8,128)(2,1)S(1)} collective-permute-done((bf16[512,1792]{1,0:T(8,128)(2,1)S(1)}, bf16[512,1792]{1,0:T(8,128)(2,1)S(1)}, u32[]{:S(2)}, u32[]{:S(2)}) %collective-permute-start.21) | collective-permute-done | bytes 1835040 | tf_op jit(solution)/shard_map/ppermute | solution.py:204
  234.3 4.7 %collective-permute-start.22 = (bf16[128,1792]{1,0:T(8,128)(2,1)S(1)}, bf16[128,1792]{1,0:T(8,128)(2,1)S(1)}, u32[]{:S(2)}, u32[]{:S(2)}) collective-permute-start(bf16[128,1792]{1,0:T(8,128)(2,1)S(1)} %get-tuple-element.130), channel_id=1, source_target_pairs={{0,8},{4,12},{1,9},{5,13},{2,10},{6,14},{3,11},{7,15}} | collective-permute-start | bytes 1376264 | tf_op jit(solution)/shard_map/ppermute | solution.py:190
  239.1 1.3 collective-permute-start.16
  241.1 8.8 %collective-permute-done.22 = bf16[128,1792]{1,0:T(8,128)(2,1)S(1)} collective-permute-done((bf16[128,1792]{1,0:T(8,128)(2,1)S(1)}, bf16[128,1792]{1,0:T(8,128)(2,1)S(1)}, u32[]{:S(2)}, u32[]{:S(2)}) %collective-permute-start.22) | collective-permute-done | bytes 458784 | tf_op jit(solution)/shard_map/ppermute | solution.py:190
  250.0 4.4 %collective-permute-start.23 = (bf16[128,1792]{1,0:T(8,128)(2,1)S(1)}, bf16[128,1792]{1,0:T(8,128)(2,1)S(1)}, u32[]{:S(2)}, u32[]{:S(2)}) collective-permute-start(bf16[128,1792]{1,0:T(8,128)(2,1)S(1)} %fusion.24), channel_id=1, source_target_pairs={{0,8},{4,12},{8,16},{12,20},{1,9},{5,13},{9,17},{13,21},{2,10},{6,... | collective-permute-start | bytes 1376264 | tf_op jit(solution)/shard_map/ppermute | solution.py:190
  254.4 5.3 %collective-permute-done.16 = bf16[128,1792]{1,0:T(8,128)(2,1)S(1)} collective-permute-done((bf16[128,1792]{1,0:T(8,128)(2,1)S(1)}, bf16[128,1792]{1,0:T(8,128)(2,1)S(1)}, u32[]{:S(2)}, u32[]{:S(2)}) %collective-permute-start.16) | collective-permute-done | bytes 458784 | tf_op jit(solution)/shard_map/ppermute | solution.py:190
  260.6 5.0 %collective-permute-start.17 = (bf16[128,1792]{1,0:T(8,128)(2,1)S(1)}, bf16[128,1792]{1,0:T(8,128)(2,1)S(1)}, u32[]{:S(2)}, u32[]{:S(2)}) collective-permute-start(bf16[128,1792]{1,0:T(8,128)(2,1)S(1)} %get-tuple-element.124), channel_id=1, source_target_pairs={{0,8},{4,12},{8,16},{12,20},{16,24},{20,28},{1,9},{5,13},{9,17},{1... | collective-permute-start | bytes 1376264 | tf_op jit(solution)/shard_map/ppermute | solution.py:190
  265.6 3.9 %collective-permute-done.23 = bf16[128,1792]{1,0:T(8,128)(2,1)S(1)} collective-permute-done((bf16[128,1792]{1,0:T(8,128)(2,1)S(1)}, bf16[128,1792]{1,0:T(8,128)(2,1)S(1)}, u32[]{:S(2)}, u32[]{:S(2)}) %collective-permute-start.23) | collective-permute-done | bytes 458784 | tf_op jit(solution)/shard_map/ppermute | solution.py:190
  271.9 9.8 %collective-permute-start.24 = (bf16[128,1792]{1,0:T(8,128)(2,1)S(1)}, bf16[128,1792]{1,0:T(8,128)(2,1)S(1)}, u32[]{:S(2)}, u32[]{:S(2)}) collective-permute-start(bf16[128,1792]{1,0:T(8,128)(2,1)S(1)} %get-tuple-element.128), channel_id=1, source_target_pairs={{0,8},{4,12},{8,16},{12,20},{16,24},{20,28},{1,9},{5,13},{9,17},{1... | collective-permute-start | bytes 1376264 | tf_op jit(solution)/shard_map/ppermute | solution.py:190
  283.1 3.8 %collective-permute-done.20 = bf16[128,1792]{1,0:T(8,128)(2,1)S(1)} collective-permute-done((bf16[128,1792]{1,0:T(8,128)(2,1)S(1)}, bf16[128,1792]{1,0:T(8,128)(2,1)S(1)}, u32[]{:S(2)}, u32[]{:S(2)}) %collective-permute-start.20) | collective-permute-done | bytes 458784 | tf_op jit(solution)/shard_map/ppermute | solution.py:190
  287.7 8.4 %collective-permute-done.27 = bf16[128,1792]{1,0:T(8,128)(2,1)S(1)} collective-permute-done((bf16[128,1792]{1,0:T(8,128)(2,1)S(1)}, bf16[128,1792]{1,0:T(8,128)(2,1)S(1)}, u32[]{:S(2)}, u32[]{:S(2)}) %collective-permute-start.27) | collective-permute-done | bytes 458784 | tf_op jit(solution)/shard_map/ppermute | solution.py:190
  (136 shorter events, 36.3 us)
Async XLA Ops:
  7.2 32.3 %all-gather.3.cloned.1.call-start = ((), (), s32[]{:S(2)}) async-start(), calls=%async_computation.1 | async-start | bytes 1310720 | tf_op jit(solution)/shard_map/all_gather | solution.py:144
  7.2 3.8 %copy-start.7 = (bf16[512,3584]{1,0:T(8,128)(2,1)S(1)}, bf16[512,3584]{1,0:T(8,128)(2,1)}, u32[]{:S(2)}) copy-start(bf16[512,3584]{1,0:T(8,128)(2,1)} %param.23) | copy-start | bytes 11010052
  11.0 1.9 copy-start.12
  11.0 2.1 copy-start.13
  13.9 3.7 %copy-start.4 = (bf16[512,896]{1,0:T(8,128)(2,1)S(1)}, bf16[512,896]{1,0:T(8,128)(2,1)}, u32[]{:S(2)}) copy-start(bf16[512,896]{1,0:T(8,128)(2,1)} %get-tuple-element.140) | copy-start | bytes 2752516
  13.9 3.7 %copy-start.5 = (bf16[512,896]{1,0:T(8,128)(2,1)S(1)}, bf16[512,896]{1,0:T(8,128)(2,1)}, u32[]{:S(2)}) copy-start(bf16[512,896]{1,0:T(8,128)(2,1)} %get-tuple-element.143) | copy-start | bytes 2752516
  13.9 3.7 %copy-start.6 = (bf16[512,896]{1,0:T(8,128)(2,1)S(1)}, bf16[512,896]{1,0:T(8,128)(2,1)}, u32[]{:S(2)}) copy-start(bf16[512,896]{1,0:T(8,128)(2,1)} %get-tuple-element.144) | copy-start | bytes 2752516
  17.6 2.9 copy-start.11
  17.6 3.1 %copy-start.17 = (s32[1,2]{1,0:T(1,128)S(1)}, s32[1,2]{1,0:T(1,128)}, u32[]{:S(2)}) copy-start(s32[1,2]{1,0:T(1,128)} %param.19) | copy-start | bytes 28
  17.6 5.2 %copy-start.14 = (bf16[1,32,512]{2,1,0:T(8,128)(2,1)S(1)}, bf16[1,32,512]{2,1,0:T(8,128)(2,1)}, u32[]{:S(2)}) copy-start(bf16[1,32,512]{2,1,0:T(8,128)(2,1)} %param.17) | copy-start | bytes 98308
  17.6 5.3 %copy-start.15 = (bf16[1,32,512]{2,1,0:T(8,128)(2,1)S(1)}, bf16[1,32,512]{2,1,0:T(8,128)(2,1)}, u32[]{:S(2)}) copy-start(bf16[1,32,512]{2,1,0:T(8,128)(2,1)} %param.18) | copy-start | bytes 98308
  19.8 45.5 %all-gather.5.cloned.1.call-start = ((), (), s32[]{:S(2)}) async-start(), calls=%async_computation.2 | async-start | bytes 1310720 | tf_op jit(solution)/shard_map/all_gather | solution.py:156
  43.9 1.6 copy-start.9
  45.5 1.8 copy-start.16
  48.4 89.9 %collective-permute-start.5 = (bf16[512,1792]{1,0:T(8,128)(2,1)}, bf16[512,1792]{1,0:T(8,128)(2,1)}, u32[]{:S(2)}, u32[]{:S(2)}) collective-permute-start(bf16[512,1792]{1,0:T(8,128)(2,1)} %get-tuple-element.102), channel_id=1, source_target_pairs={{0,4},{4,0},{8,12},{12,8},{16,20},{20,16},{24,28},{28,24},{1,5},{5... | collective-permute-start | bytes 5505032 | tf_op jit(solution)/shard_map/ppermute | solution.py:113
  49.9 80.3 %collective-permute-start = (bf16[512,1792]{1,0:T(8,128)(2,1)}, bf16[512,1792]{1,0:T(8,128)(2,1)}, u32[]{:S(2)}, u32[]{:S(2)}) collective-permute-start(bf16[512,1792]{1,0:T(8,128)(2,1)} %get-tuple-element.88), channel_id=1, source_target_pairs={{0,4},{4,0},{8,12},{12,8},{16,20},{20,16},{24,28},{28,24},{1,5},{5... | collective-permute-start | bytes 5505032 | tf_op jit(solution)/shard_map/ppermute | solution.py:113
  67.6 30.8 %all-to-all-start = ((bf16[4,128,1024]{2,1,0:T(8,128)(2,1)}), bf16[4,128,1024]{2,1,0:T(8,128)(2,1)}, u32[]{:S(2)}, u32[]{:S(2)}) async-start(bf16[4,128,1024]{2,1,0:T(8,128)(2,1)} %bitcast.261), calls=%async_computation | async-start | bytes 2097152 | tf_op jit(solution)/shard_map/all_to_all | solution.py:161
  72.2 5.8 %copy-start = (f32[4,512,1024]{2,1,0:T(8,128)S(1)}, f32[4,512,1024]{2,1,0:T(8,128)}, u32[]{:S(2)}) copy-start(f32[4,512,1024]{2,1,0:T(8,128)} %get-tuple-element.158) | copy-start | bytes 25165828
  72.2 5.9 %copy-start.10 = (bf16[512,4,128]{2,0,1:T(8,128)(2,1)S(1)}, bf16[512,4,128]{2,0,1:T(8,128)(2,1)}, u32[]{:S(2)}) copy-start(bf16[512,4,128]{2,0,1:T(8,128)(2,1)} %copy.26) | copy-start | bytes 1572868
  100.2 2.4 copy-start.3
  103.8 33.3 %copy-start.2 = (bf16[512,1792]{1,0:T(8,128)(2,1)S(1)}, bf16[512,1792]{1,0:T(8,128)(2,1)}, u32[]{:S(2)}) copy-start(bf16[512,1792]{1,0:T(8,128)(2,1)} %get-tuple-element.102) | copy-start | bytes 5505028
  133.0 14.4 %collective-permute-start.1 = (bf16[128,1792]{1,0:T(8,128)(2,1)S(1)}, bf16[128,1792]{1,0:T(8,128)(2,1)S(1)}, u32[]{:S(2)}, u32[]{:S(2)}) collective-permute-start(bf16[128,1792]{1,0:T(8,128)(2,1)S(1)} %get-tuple-element.137), channel_id=1, source_target_pairs={{0,8},{4,12},{1,9},{5,13},{2,10},{6,14},{3,11},{7,15}} | collective-permute-start | bytes 1376264 | tf_op jit(solution)/shard_map/ppermute | solution.py:190
  136.4 10.9 %collective-permute-start.2 = (bf16[128,1792]{1,0:T(8,128)(2,1)S(1)}, bf16[128,1792]{1,0:T(8,128)(2,1)S(1)}, u32[]{:S(2)}, u32[]{:S(2)}) collective-permute-start(bf16[128,1792]{1,0:T(8,128)(2,1)S(1)} %get-tuple-element.136), channel_id=1, source_target_pairs={{24,16},{28,20},{25,17},{29,21},{26,18},{30,22},{27,19},{31,23}} | collective-permute-start | bytes 1376264 | tf_op jit(solution)/shard_map/ppermute | solution.py:190
  140.9 12.0 %copy-start.1 = (bf16[512,1792]{1,0:T(8,128)(2,1)S(1)}, bf16[512,1792]{1,0:T(8,128)(2,1)}, u32[]{:S(2)}) copy-start(bf16[512,1792]{1,0:T(8,128)(2,1)} %get-tuple-element.107) | copy-start | bytes 5505028
  141.0 16.2 %collective-permute-start.6 = (bf16[128,1792]{1,0:T(8,128)(2,1)S(1)}, bf16[128,1792]{1,0:T(8,128)(2,1)S(1)}, u32[]{:S(2)}, u32[]{:S(2)}) collective-permute-start(bf16[128,1792]{1,0:T(8,128)(2,1)S(1)} %get-tuple-element.133), channel_id=1, source_target_pairs={{0,8},{4,12},{1,9},{5,13},{2,10},{6,14},{3,11},{7,15}} | collective-permute-start | bytes 1376264 | tf_op jit(solution)/shard_map/ppermute | solution.py:190
  142.5 14.7 %collective-permute-start.7 = (bf16[128,1792]{1,0:T(8,128)(2,1)S(1)}, bf16[128,1792]{1,0:T(8,128)(2,1)S(1)}, u32[]{:S(2)}, u32[]{:S(2)}) collective-permute-start(bf16[128,1792]{1,0:T(8,128)(2,1)S(1)} %get-tuple-element.132), channel_id=1, source_target_pairs={{24,16},{28,20},{25,17},{29,21},{26,18},{30,22},{27,19},{31,23}} | collective-permute-start | bytes 1376264 | tf_op jit(solution)/shard_map/ppermute | solution.py:190
  147.5 17.9 %collective-permute-start.3 = (bf16[128,1792]{1,0:T(8,128)(2,1)S(1)}, bf16[128,1792]{1,0:T(8,128)(2,1)S(1)}, u32[]{:S(2)}, u32[]{:S(2)}) collective-permute-start(bf16[128,1792]{1,0:T(8,128)(2,1)S(1)} %get-tuple-element.135), channel_id=1, source_target_pairs={{0,8},{4,12},{8,16},{12,20},{1,9},{5,13},{9,17},{13,21},{2,10},{6,... | collective-permute-start | bytes 1376264 | tf_op jit(solution)/shard_map/ppermute | solution.py:190
  151.9 13.5 %collective-permute-start.4 = (bf16[128,1792]{1,0:T(8,128)(2,1)S(1)}, bf16[128,1792]{1,0:T(8,128)(2,1)S(1)}, u32[]{:S(2)}, u32[]{:S(2)}) collective-permute-start(bf16[128,1792]{1,0:T(8,128)(2,1)S(1)} %get-tuple-element.134), channel_id=1, source_target_pairs={{16,8},{20,12},{24,16},{28,20},{17,9},{21,13},{25,17},{29,21},{18,... | collective-permute-start | bytes 1376264 | tf_op jit(solution)/shard_map/ppermute | solution.py:190
  155.1 43.0 %collective-permute-start.14 = (bf16[512,1792]{1,0:T(8,128)(2,1)S(1)}, bf16[512,1792]{1,0:T(8,128)(2,1)S(1)}, u32[]{:S(2)}, u32[]{:S(2)}) collective-permute-start(bf16[512,1792]{1,0:T(8,128)(2,1)S(1)} %copy-done.1), channel_id=1, source_target_pairs={{0,4},{4,0},{8,12},{12,8},{16,20},{20,16},{24,28},{28,24},{1,5},{5... | collective-permute-start | bytes 5505032 | tf_op jit(solution)/shard_map/ppermute | solution.py:204
  165.5 15.3 %collective-permute-start.10 = (bf16[128,1792]{1,0:T(8,128)(2,1)S(1)}, bf16[128,1792]{1,0:T(8,128)(2,1)S(1)}, u32[]{:S(2)}, u32[]{:S(2)}) collective-permute-start(bf16[128,1792]{1,0:T(8,128)(2,1)S(1)} %fusion.34), channel_id=1, source_target_pairs={{0,8},{4,12},{8,16},{12,20},{1,9},{5,13},{9,17},{13,21},{2,10},{6,... | collective-permute-start | bytes 1376264 | tf_op jit(solution)/shard_map/ppermute | solution.py:190
  170.1 18.0 %collective-permute-start.8 = (bf16[128,1792]{1,0:T(8,128)(2,1)S(1)}, bf16[128,1792]{1,0:T(8,128)(2,1)S(1)}, u32[]{:S(2)}, u32[]{:S(2)}) collective-permute-start(bf16[128,1792]{1,0:T(8,128)(2,1)S(1)} %get-tuple-element.120), channel_id=1, source_target_pairs={{0,8},{4,12},{8,16},{12,20},{16,24},{20,28},{1,9},{5,13},{9,17},{1... | collective-permute-start | bytes 1376264 | tf_op jit(solution)/shard_map/ppermute | solution.py:190
  174.2 18.4 %collective-permute-start.9 = (bf16[128,1792]{1,0:T(8,128)(2,1)S(1)}, bf16[128,1792]{1,0:T(8,128)(2,1)S(1)}, u32[]{:S(2)}, u32[]{:S(2)}) collective-permute-start(bf16[128,1792]{1,0:T(8,128)(2,1)S(1)} %get-tuple-element.121), channel_id=1, source_target_pairs={{8,0},{12,4},{16,8},{20,12},{24,16},{28,20},{9,1},{13,5},{17,9},{2... | collective-permute-start | bytes 1376264 | tf_op jit(solution)/shard_map/ppermute | solution.py:190
  175.5 57.5 %collective-permute-start.21 = (bf16[512,1792]{1,0:T(8,128)(2,1)S(1)}, bf16[512,1792]{1,0:T(8,128)(2,1)S(1)}, u32[]{:S(2)}, u32[]{:S(2)}) collective-permute-start(bf16[512,1792]{1,0:T(8,128)(2,1)S(1)} %get-tuple-element.108), channel_id=1, source_target_pairs={{0,4},{4,0},{8,12},{12,8},{16,20},{20,16},{24,28},{28,24},{1,5},{5... | collective-permute-start | bytes 5505032 | tf_op jit(solution)/shard_map/ppermute | solution.py:204
  181.0 11.8 %collective-permute-start.12 = (bf16[128,1792]{1,0:T(8,128)(2,1)S(1)}, bf16[128,1792]{1,0:T(8,128)(2,1)S(1)}, u32[]{:S(2)}, u32[]{:S(2)}) collective-permute-start(bf16[128,1792]{1,0:T(8,128)(2,1)S(1)} %get-tuple-element.123), channel_id=1, source_target_pairs={{16,8},{20,12},{24,16},{28,20},{17,9},{21,13},{25,17},{29,21},{18,... | collective-permute-start | bytes 1376264 | tf_op jit(solution)/shard_map/ppermute | solution.py:190
  188.1 16.6 %collective-permute-start.11 = (bf16[128,1792]{1,0:T(8,128)(2,1)S(1)}, bf16[128,1792]{1,0:T(8,128)(2,1)S(1)}, u32[]{:S(2)}, u32[]{:S(2)}) collective-permute-start(bf16[128,1792]{1,0:T(8,128)(2,1)S(1)} %get-tuple-element.122), channel_id=1, source_target_pairs={{0,8},{4,12},{8,16},{12,20},{16,24},{20,28},{1,9},{5,13},{9,17},{1... | collective-permute-start | bytes 1376264 | tf_op jit(solution)/shard_map/ppermute | solution.py:190
  193.0 13.6 %collective-permute-start.13 = (bf16[128,1792]{1,0:T(8,128)(2,1)S(1)}, bf16[128,1792]{1,0:T(8,128)(2,1)S(1)}, u32[]{:S(2)}, u32[]{:S(2)}) collective-permute-start(bf16[128,1792]{1,0:T(8,128)(2,1)S(1)} %fusion.33), channel_id=1, source_target_pairs={{8,0},{12,4},{16,8},{20,12},{24,16},{28,20},{9,1},{13,5},{17,9},{2... | collective-permute-start | bytes 1376264 | tf_op jit(solution)/shard_map/ppermute | solution.py:190
  199.4 39.6 %collective-permute-start.15 = (bf16[128,1792]{1,0:T(8,128)(2,1)S(1)}, bf16[128,1792]{1,0:T(8,128)(2,1)S(1)}, u32[]{:S(2)}, u32[]{:S(2)}) collective-permute-start(bf16[128,1792]{1,0:T(8,128)(2,1)S(1)} %get-tuple-element.126), channel_id=1, source_target_pairs={{0,8},{4,12},{1,9},{5,13},{2,10},{6,14},{3,11},{7,15}} | collective-permute-start | bytes 1376264 | tf_op jit(solution)/shard_map/ppermute | solution.py:190
  204.1 50.3 %collective-permute-start.18 = (bf16[128,1792]{1,0:T(8,128)(2,1)S(1)}, bf16[128,1792]{1,0:T(8,128)(2,1)S(1)}, u32[]{:S(2)}, u32[]{:S(2)}) collective-permute-start(bf16[128,1792]{1,0:T(8,128)(2,1)S(1)} %get-tuple-element.127), channel_id=1, source_target_pairs={{24,16},{28,20},{25,17},{29,21},{26,18},{30,22},{27,19},{31,23}} | collective-permute-start | bytes 1376264 | tf_op jit(solution)/shard_map/ppermute | solution.py:190
  234.3 15.6 %collective-permute-start.22 = (bf16[128,1792]{1,0:T(8,128)(2,1)S(1)}, bf16[128,1792]{1,0:T(8,128)(2,1)S(1)}, u32[]{:S(2)}, u32[]{:S(2)}) collective-permute-start(bf16[128,1792]{1,0:T(8,128)(2,1)S(1)} %get-tuple-element.130), channel_id=1, source_target_pairs={{0,8},{4,12},{1,9},{5,13},{2,10},{6,14},{3,11},{7,15}} | collective-permute-start | bytes 1376264 | tf_op jit(solution)/shard_map/ppermute | solution.py:190
  239.1 20.7 %collective-permute-start.16 = (bf16[128,1792]{1,0:T(8,128)(2,1)S(1)}, bf16[128,1792]{1,0:T(8,128)(2,1)S(1)}, u32[]{:S(2)}, u32[]{:S(2)}) collective-permute-start(bf16[128,1792]{1,0:T(8,128)(2,1)S(1)} %fusion.29), channel_id=1, source_target_pairs={{0,8},{4,12},{8,16},{12,20},{1,9},{5,13},{9,17},{13,21},{2,10},{6,... | collective-permute-start | bytes 1376264 | tf_op jit(solution)/shard_map/ppermute | solution.py:190
  240.4 25.3 %collective-permute-start.25 = (bf16[128,1792]{1,0:T(8,128)(2,1)S(1)}, bf16[128,1792]{1,0:T(8,128)(2,1)S(1)}, u32[]{:S(2)}, u32[]{:S(2)}) collective-permute-start(bf16[128,1792]{1,0:T(8,128)(2,1)S(1)} %get-tuple-element.131), channel_id=1, source_target_pairs={{24,16},{28,20},{25,17},{29,21},{26,18},{30,22},{27,19},{31,23}} | collective-permute-start | bytes 1376264 | tf_op jit(solution)/shard_map/ppermute | solution.py:190
  250.0 19.6 %collective-permute-start.23 = (bf16[128,1792]{1,0:T(8,128)(2,1)S(1)}, bf16[128,1792]{1,0:T(8,128)(2,1)S(1)}, u32[]{:S(2)}, u32[]{:S(2)}) collective-permute-start(bf16[128,1792]{1,0:T(8,128)(2,1)S(1)} %fusion.24), channel_id=1, source_target_pairs={{0,8},{4,12},{8,16},{12,20},{1,9},{5,13},{9,17},{13,21},{2,10},{6,... | collective-permute-start | bytes 1376264 | tf_op jit(solution)/shard_map/ppermute | solution.py:190
  259.9 10.5 %collective-permute-start.19 = (bf16[128,1792]{1,0:T(8,128)(2,1)S(1)}, bf16[128,1792]{1,0:T(8,128)(2,1)S(1)}, u32[]{:S(2)}, u32[]{:S(2)}) collective-permute-start(bf16[128,1792]{1,0:T(8,128)(2,1)S(1)} %get-tuple-element.125), channel_id=1, source_target_pairs={{16,8},{20,12},{24,16},{28,20},{17,9},{21,13},{25,17},{29,21},{18,... | collective-permute-start | bytes 1376264 | tf_op jit(solution)/shard_map/ppermute | solution.py:190
  260.6 22.5 %collective-permute-start.17 = (bf16[128,1792]{1,0:T(8,128)(2,1)S(1)}, bf16[128,1792]{1,0:T(8,128)(2,1)S(1)}, u32[]{:S(2)}, u32[]{:S(2)}) collective-permute-start(bf16[128,1792]{1,0:T(8,128)(2,1)S(1)} %get-tuple-element.124), channel_id=1, source_target_pairs={{0,8},{4,12},{8,16},{12,20},{16,24},{20,28},{1,9},{5,13},{9,17},{1... | collective-permute-start | bytes 1376264 | tf_op jit(solution)/shard_map/ppermute | solution.py:190
  269.8 12.0 %collective-permute-start.26 = (bf16[128,1792]{1,0:T(8,128)(2,1)S(1)}, bf16[128,1792]{1,0:T(8,128)(2,1)S(1)}, u32[]{:S(2)}, u32[]{:S(2)}) collective-permute-start(bf16[128,1792]{1,0:T(8,128)(2,1)S(1)} %get-tuple-element.129), channel_id=1, source_target_pairs={{16,8},{20,12},{24,16},{28,20},{17,9},{21,13},{25,17},{29,21},{18,... | collective-permute-start | bytes 1376264 | tf_op jit(solution)/shard_map/ppermute | solution.py:190
  270.6 16.4 %collective-permute-start.20 = (bf16[128,1792]{1,0:T(8,128)(2,1)S(1)}, bf16[128,1792]{1,0:T(8,128)(2,1)S(1)}, u32[]{:S(2)}, u32[]{:S(2)}) collective-permute-start(bf16[128,1792]{1,0:T(8,128)(2,1)S(1)} %fusion.28), channel_id=1, source_target_pairs={{8,0},{12,4},{16,8},{20,12},{24,16},{28,20},{9,1},{13,5},{17,9},{2... | collective-permute-start | bytes 1376264 | tf_op jit(solution)/shard_map/ppermute | solution.py:190
  271.9 15.8 %collective-permute-start.24 = (bf16[128,1792]{1,0:T(8,128)(2,1)S(1)}, bf16[128,1792]{1,0:T(8,128)(2,1)S(1)}, u32[]{:S(2)}, u32[]{:S(2)}) collective-permute-start(bf16[128,1792]{1,0:T(8,128)(2,1)S(1)} %get-tuple-element.128), channel_id=1, source_target_pairs={{0,8},{4,12},{8,16},{12,20},{16,24},{20,28},{1,9},{5,13},{9,17},{1... | collective-permute-start | bytes 1376264 | tf_op jit(solution)/shard_map/ppermute | solution.py:190
  281.8 14.2 %collective-permute-start.27 = (bf16[128,1792]{1,0:T(8,128)(2,1)S(1)}, bf16[128,1792]{1,0:T(8,128)(2,1)S(1)}, u32[]{:S(2)}, u32[]{:S(2)}) collective-permute-start(bf16[128,1792]{1,0:T(8,128)(2,1)S(1)} %fusion.23), channel_id=1, source_target_pairs={{8,0},{12,4},{16,8},{20,12},{24,16},{28,20},{9,1},{13,5},{17,9},{2... | collective-permute-start | bytes 1376264 | tf_op jit(solution)/shard_map/ppermute | solution.py:190
  (1 other events, 1.4 us)
Sparse Core Ops, SparseCore 0:
  19.9 19.5 all-gather.2
  48.5 16.7 all-gather.4
